TPU v7x, 32 devices: a whole 2x2x4 slice. The times are simulated.
32 devices in a mesh: grp: 2 (over y), chan: 4 (over z), tm: 2 (over x), blk: 2 (over core).
Axes of the slice: x: 2, y: 2, z: 4, core: 2. Of those that a mesh axis runs over, the one named last changes fastest.
Arguments:
- samples: bfloat16 [32, 2048, 2048], P('tm', ('grp', 'chan', 'blk')), parts along dimension 1, may hold values from -6 to 6
- channel_gains: float32 [2, 1024, 1024], P(None, None, ('chan', 'blk')), may hold values from -4 to 4
- block_pairs: int32 [4, 2], P('blk'), may hold values from 0 to 7, as said below
Outputs:
- visibilities: float32 [2, 2048, 4, 128, 128], P(None, ('grp', 'chan', 'tm'), 'blk'), parts along dimension 1
There are 2 independent parts, one for each index of `grp`. A program takes and returns all parts, laid end to end along the dimension named above; an argument that names none is the same for every part. Nothing has to cross between parts.
Inputs may be any that keep to these rules, and one draw needn't show every extreme that they name: `block_pairs`: each row holds two different input blocks, the smaller first; each of the 8 blocks appears in exactly one row.
All inputs are finite; a program needn't handle non-finite values.
Results may differ from a plain program's by a relative error of at most 0.0071.
Values may be sent and summed in bfloat16 or wider, within the bound.
A program may use at most 192 MiB of HBM per device.

v0:
```python
import math

import jax
import jax.numpy as jnp
from jax import lax
from jax.sharding import PartitionSpec as P

NCH = 1024
TAPS = 16
BLOCK = 128


def passed_along(block, axis, distance):
    devices = range(lax.axis_size(axis))
    route = [(i - distance, i) for i in devices if i - distance in devices]
    return lax.ppermute(block, axis, route)


def filter_window(tap_count, frame_len):
    position = jnp.arange(tap_count * frame_len, dtype=jnp.int32).astype(jnp.float32)
    offset = (position + 0.5) / frame_len - tap_count / 2.0
    prototype = jnp.sin(jnp.pi * offset) / (jnp.pi * offset)
    prototype = prototype * (
        0.5 - 0.5 * jnp.cos(2.0 * jnp.pi * (position + 0.5) / (tap_count * frame_len))
    )
    return prototype.reshape(tap_count, frame_len)[::-1]


def channel_table(frame_len, chan_count):
    chan_idx = jnp.arange(chan_count, dtype=jnp.int32)[:, None]
    sample_idx = jnp.arange(frame_len, dtype=jnp.int32)[None, :]
    phase_angle = (sample_idx * chan_idx % frame_len).astype(jnp.float32) * (
        2.0 * math.pi / frame_len
    )
    norm_scale = 1.0 / math.sqrt(frame_len)
    return jnp.concatenate(
        [jnp.cos(phase_angle) * norm_scale, -jnp.sin(phase_angle) * norm_scale], 0
    ).astype(jnp.bfloat16)


def shards(samples, channel_gains, block_pairs):
    spectra_dev, inputs_dev, frame_len = samples.shape
    rim_frames = passed_along(samples[spectra_dev - (TAPS - 1) :], "tm", 1)
    padded = jnp.concatenate([rim_frames, samples], 0)
    window = filter_window(TAPS, frame_len)
    filtered = jnp.zeros((spectra_dev, inputs_dev, frame_len), jnp.float32)
    for tap in range(TAPS):
        filtered = filtered + window[tap] * padded[
            TAPS - 1 - tap : TAPS - 1 - tap + spectra_dev
        ].astype(jnp.float32)
    filtered = filtered.astype(jnp.bfloat16).reshape(spectra_dev * inputs_dev, frame_len)
    dft_table = channel_table(frame_len, NCH)
    spectrum = lax.dot_general(
        dft_table, filtered, (((1,), (1,)), ((), ())), preferred_element_type=jnp.float32
    )
    spectrum = spectrum.reshape(2, NCH, spectra_dev, inputs_dev)
    gain_real = channel_gains[0][:, None, :]
    gain_imag = channel_gains[1][:, None, :]
    volts = jnp.stack(
        [
            spectrum[0] * gain_real - spectrum[1] * gain_imag,
            spectrum[0] * gain_imag + spectrum[1] * gain_real,
        ],
        0,
    ).astype(jnp.bfloat16)
    n_chan = lax.axis_size("chan")
    n_time = lax.axis_size("tm")
    moved_parts = lax.all_to_all(
        volts[None], ("chan", "tm"), split_axis=2, concat_axis=0, tiled=True
    )
    chans_dev = moved_parts.shape[2]
    moved_parts = moved_parts.reshape(n_chan, n_time, 2, chans_dev, spectra_dev, inputs_dev)
    slab_volts = jnp.transpose(moved_parts, (2, 3, 1, 4, 0, 5)).reshape(
        2, chans_dev, n_time * spectra_dev, n_chan * inputs_dev
    )
    chans_dev = slab_volts.shape[1]
    time_count = slab_volts.shape[2]
    halves = lax.all_gather(slab_volts[:, :, :, None, :], "blk", axis=3, tiled=True)
    n_halves = halves.shape[3]
    all_inputs = halves.reshape(2, chans_dev, time_count, n_halves, n_chan, inputs_dev)
    all_inputs = jnp.transpose(all_inputs, (0, 1, 2, 4, 3, 5)).reshape(
        2, chans_dev, time_count, n_halves * n_chan * inputs_dev
    )
    norm_scale = 1.0 / math.sqrt(time_count)
    results = []
    for pair_slot in range(block_pairs.shape[0]):
        first_block = lax.dynamic_slice_in_dim(
            all_inputs, block_pairs[pair_slot, 0] * BLOCK, BLOCK, 3
        )
        second_block = lax.dynamic_slice_in_dim(
            all_inputs, block_pairs[pair_slot, 1] * BLOCK, BLOCK, 3
        )
        real_part = jnp.einsum(
            "rctp,rctq->cpq", first_block, second_block, preferred_element_type=jnp.float32
        )
        turned = jnp.stack([first_block[1], -first_block[0]], 0)
        imag_part = jnp.einsum(
            "rctp,rctq->cpq", turned, second_block, preferred_element_type=jnp.float32
        )
        results.append(jnp.stack([real_part, imag_part], 0) * norm_scale)
    return jnp.stack(results, 2)


def solution(mesh):
    placed = (P("tm", ("grp", "chan", "blk"), None), P(None, None, ("chan", "blk")), P("blk", None))
    return jax.shard_map(
        shards,
        mesh=mesh,
        in_specs=placed,
        out_specs=P(None, ("grp", "chan", "tm"), "blk", None, None),
        check_vma=False,
    )
```

profile of v0, /device:TPU:19, one launch (start us, length us, event | category | flops | bytes accessed | tf_op | source)
XLA Modules:
  0.0 733.1 jit_solution(6475358482870549556)
XLA Ops:
  6.5 0.0 all-gather.2.cloned.1.call-start
  6.5 8.0 %slice.154 = bf16[15,128,2048]{2,1,0:T(8,128)(2,1)} slice(bf16[16,128,2048]{2,1,0:T(8,128)(2,1)} %param.3), slice={[1:16], [0:128], [0:2048]} | slice | bytes 15728640 | tf_op jit(solution)/shard_map/slice | solution.py:43
  14.5 1.3 collective-permute-start
  15.8 0.9 fusion.24
  16.7 1.3 slice_bitcast_fusion.1
  18.0 0.1 fusion.33
  18.1 35.0 %multiply_convert_fusion = (bf16[1024,2048]{1,0:T(8,128)(2,1)}, bf16[1024,2048]{1,0:T(8,128)(2,1)}) fusion(), kind=kLoop, calls=%fused_computation.17 | loop fusion | flops 39845888 | bytes 8388608 | tf_op jit(solution)/shard_map/convert.5
  53.1 133.6 %collective-permute-done = bf16[15,128,2048]{2,1,0:T(8,128)(2,1)S(1)} collective-permute-done((bf16[15,128,2048]{2,1,0:T(8,128)(2,1)}, bf16[15,128,2048]{2,1,0:T(8,128)(2,1)S(1)}, u32[]{:S(2)}, u32[]{:S(2)}) %collective-permute-start) | collective-permute-done | bytes 7864352 | tf_op jit(solution)/shard_map/ppermute | solution.py:16
  186.7 4.2 constant_dynamic-update-slice_fusion.1
  190.9 8.4 %constant_dynamic-update-slice_fusion = bf16[31,128,2048]{2,1,0:T(8,128)(2,1)} fusion(bf16[31,128,2048]{2,1,0:T(8,128)(2,1)} %constant_dynamic-update-slice_fusion.1, bf16[16,128,2048]{2,1,0:T(8,128)(2,1)} %param.3), kind=kLoop, calls=%fused_computation.46 | loop fusion | bytes 16777216 | tf_op jit(solution)/shard_map/concatenate | solution.py:44
  199.4 0.0 copy-start.2
  199.4 57.9 %add_convert_fusion = bf16[16,128,2048]{2,1,0:T(8,128)(2,1)} fusion(bf16[16,128,2048]{2,1,0:T(8,128)(2,1)} %param.3, bf16[31,128,2048]{2,1,0:T(8,128)(2,1)} %constant_dynamic-update-slice_fusion, f32[2048]{0:T(1024)S(1)} %bitcast.75, f32[2048]{0:T(1024)S(1)} %bitcast.76, f32[2048]{0:T(1024)S(1)} %bitcast.77, f32[2048]{0:T(1024)S(1)} %bitcast.78, ...), kind=kLoop, calls=%fused_computation.3 | loop fusion | flops 201326592 | bytes 142737408 | tf_op jit(solution)/shard_map/convert_element_type | solution.py:51
  257.2 0.0 copy-done.2
  257.2 21.4 %fusion.3 = f32[2048,2048]{0,1:T(8,128)S(1)} fusion(bf16[2048,2048]{1,0:T(8,128)(2,1)} %bitcast.73, bf16[1024,2048]{1,0:T(8,128)(2,1)S(1)} %copy-done.2, bf16[1024,2048]{1,0:T(8,128)(2,1)} %get-tuple-element.36), kind=kOutput, calls=%fused_computation.10 | convolution fusion | flops 17196646400 | bytes 33554432 | tf_op jit(solution)/shard_map/dot_general | solution.py:53
  278.7 6.7 fusion.32
  285.4 9.2 %copy.27 = f32[1,1024,16,128]{3,2,1,0:T(8,128)} copy(f32[1,1024,16,128]{1,3,2,0:T(8,128)} %bitcast.72) | data formatting | bytes 16777216 | tf_op jit(solution)/shard_map/squeeze | solution.py:61
  294.6 9.1 %copy.28 = f32[1,1024,16,128]{3,2,1,0:T(8,128)} copy(f32[1,1024,16,128]{1,3,2,0:T(8,128)} %bitcast.71) | data formatting | bytes 16777216 | tf_op jit(solution)/shard_map/squeeze | solution.py:61
  303.7 8.6 %fusion.10 = (bf16[1,1,1024,16,128]{4,3,1,0,2:T(8,128)(2,1)S(1)}, bf16[1,1,1024,16,128]{4,3,1,0,2:T(8,128)(2,1)}) fusion(f32[1,1024,16,128]{3,2,1,0:T(8,128)} %copy.28, f32[1,1024,16,128]{3,2,1,0:T(8,128)} %copy.27, f32[1024,128]{1,0:T(8,128)S(1)} %get-tuple-element.14, f32[1024,128]{1,0:T(8,128)S(1)} %get-tuple-element.13), kind=kLoop, calls=%fused_computation.22 | loop fusion | flops 16777216 | bytes 26214400 | tf_op jit(solution)/shard_map/stack | solution.py:59
  312.3 6.3 pad_maximum_fusion.1
  318.6 185.5 %all_to_all.15 = bf16[1,2,1024,16,128]{4,3,1,0,2:T(8,128)(2,1)} all-to-all(bf16[1,2,1024,16,128]{4,3,1,0,2:T(8,128)(2,1)} %pad_maximum_fusion.1), channel_id=1, replica_groups=mesh['grp'=2,'chan'=4,'tm'=2,'blk'=2] {'chan','tm'}, dimensions={2} | all-to-all | bytes 16777216 | tf_op jit(solution)/shard_map/all_to_all | solution.py:68
  504.1 14.0 %copy.34 = bf16[2,128,2,16,4,128]{1,5,4,3,2,0:T(8,128)(2,1)} copy(bf16[2,128,2,16,4,128]{5,3,0,1,2,4:T(8,128)(2,1)} %bitcast.69) | data formatting | bytes 16777216 | tf_op jit(solution)/shard_map/transpose | solution.py:73
  518.1 14.6 %copy.35 = bf16[2,128,32,1,512]{4,2,1,0,3:T(8,128)(2,1)} copy(bf16[2,128,32,1,512]{1,4,2,0,3:T(8,128)(2,1)} %bitcast.70) | data formatting | bytes 16777216 | tf_op jit(solution)/shard_map/broadcast_in_dim;reshape | solution.py:78
  532.8 0.0 copy-start.3
  532.8 0.0 all-gather.2.cloned.1.call-update
  532.8 0.7 copy-done.3
  533.5 0.6 fusion.34
  536.6 29.6 %all-gather.2.cloned.1.call-done = bf16[2,128,32,2,512]{4,2,1,0,3:T(8,128)(2,1)} async-done(((bf16[2,128,32,1,512]{4,2,1,0,3:T(8,128)(2,1)}), bf16[2,128,32,2,512]{4,2,1,0,3:T(8,128)(2,1)}) %all-gather.2.cloned.1.call-update) | async-done | bytes 16777232 | tf_op jit(solution)/shard_map/all_gather | solution.py:78
  566.1 28.1 %copy.36 = bf16[2,128,32,2,512]{1,4,3,2,0:T(8,128)(2,1)} copy(bf16[2,128,32,2,512]{4,2,1,0,3:T(8,128)(2,1)} %all-gather.2.cloned.1.call-done) | data formatting | bytes 33554432 | tf_op jit(solution)/shard_map/all_gather | solution.py:78
  594.2 41.2 %copy.37 = bf16[2,128,32,4,2,128]{5,4,3,2,0,1:T(2,128)(2,1)} copy(bf16[2,128,32,4,2,128]{1,5,3,4,2,0:T(8,128)(2,1)} %bitcast.68) | data formatting | bytes 33554432 | tf_op jit(solution)/shard_map/transpose | solution.py:81
  635.4 27.4 %reshape.200 = bf16[2,128,32,1024]{3,2,0,1:T(8,128)(2,1)} reshape(bf16[2,128,32,4,2,128]{5,4,3,2,0,1:T(2,128)(2,1)} %copy.37) | data formatting | bytes 33554432 | tf_op jit(solution)/shard_map/reshape | solution.py:81
  662.8 0.0 copy-start
  662.8 3.7 convolution_bitcast_fusion.1
  666.5 4.9 constant_dynamic-slice_fusion.1
  671.4 0.9 copy-done
  672.3 1.3 convolution_bitcast_fusion.3
  673.6 6.1 convolution_bitcast_fusion.2
  679.7 6.0 convolution_bitcast_fusion
  685.7 0.0 copy-start.1
  685.7 10.6 %maximum_multiply_fusion = f32[2,128,1,128,128]{4,3,1,2,0:T(8,128)} fusion(f32[1,128,1,128,128]{4,3,1,2,0:T(8,128)} %convolution_bitcast_fusion.2, f32[1,128,1,128,128]{4,3,1,2,0:T(8,128)S(1)} %convolution_bitcast_fusion.3), kind=kLoop, calls=%fused_computation.1 | loop fusion | flops 8388608 | bytes 33554432 | tf_op jit(solution)/shard_map/mul | solution.py:100
  696.3 0.1 copy-done.1
  696.5 6.4 maximum_multiply_fusion.1
  702.9 12.1 %pad_maximum_fusion = f32[2,128,2,128,128]{4,3,1,2,0:T(8,128)S(1)} fusion(f32[2,128,1,128,128]{4,3,1,2,0:T(8,128)} %maximum_multiply_fusion.1, f32[2,128,1,128,128]{4,3,1,2,0:T(8,128)} %maximum_multiply_fusion), kind=kLoop, calls=%fused_computation | loop fusion | flops 8388608 | bytes 67108864 | tf_op jit(solution)/shard_map/stack | solution.py:101
  715.0 11.3 %copy.38 = f32[2,128,2,128,128]{4,3,2,1,0:T(8,128)} copy(f32[2,128,2,128,128]{4,3,1,2,0:T(8,128)S(1)} %pad_maximum_fusion) | data formatting | bytes 67108864 | tf_op jit(solution)/shard_map/stack | solution.py:101
Async XLA Ops:
  6.5 559.6 %all-gather.2.cloned.1.call-start = ((), (), s32[]{:S(2)}) async-start(), calls=%async_computation.1 | async-start | bytes 25165824 | tf_op jit(solution)/shard_map/all_gather | solution.py:78
  14.5 172.2 %collective-permute-start = (bf16[15,128,2048]{2,1,0:T(8,128)(2,1)}, bf16[15,128,2048]{2,1,0:T(8,128)(2,1)S(1)}, u32[]{:S(2)}, u32[]{:S(2)}) collective-permute-start(bf16[15,128,2048]{2,1,0:T(8,128)(2,1)} %slice.154), channel_id=1, source_target_pairs={{0,2},{1,3},{4,6},{5,7},{8,10},{9,11},{12,14},{13,15},{16,18},{17,... | collective-permute-start | bytes 23592968 | tf_op jit(solution)/shard_map/ppermute | solution.py:16
  199.4 57.9 %copy-start.2 = (bf16[1024,2048]{1,0:T(8,128)(2,1)S(1)}, bf16[1024,2048]{1,0:T(8,128)(2,1)}, u32[]{:S(2)}) copy-start(bf16[1024,2048]{1,0:T(8,128)(2,1)} %get-tuple-element.35) | copy-start | bytes 12582916
  532.8 0.7 copy-start.3
  662.8 9.5 %copy-start = (bf16[2,128,32,1024]{3,2,0,1:T(8,128)(2,1)S(1)}, bf16[2,128,32,1024]{3,2,0,1:T(8,128)(2,1)}, u32[]{:S(2)}) copy-start(bf16[2,128,32,1024]{3,2,0,1:T(8,128)(2,1)} %reshape.200) | copy-start | bytes 50331652
  685.7 10.8 %copy-start.1 = (f32[1,128,1,128,128]{4,3,1,2,0:T(8,128)S(1)}, f32[1,128,1,128,128]{4,3,1,2,0:T(8,128)}, u32[]{:S(2)}) copy-start(f32[1,128,1,128,128]{4,3,1,2,0:T(8,128)} %convolution_bitcast_fusion) | copy-start | bytes 25165828
Sparse Core Ops, SparseCore 0:
  532.9 33.1 all-gather.1
where the time goes:
time: 738 us; the launch traced here: 733 us
  local copies, waits for them, and re-layouts  186 us (25%)
  blocking collectives  186 us (25%)
  waiting for transfers between devices  163 us (22%)
  other arithmetic  143 us (19%)
  matrix products  38.6 us (5%)
  between operations  16 us (2%)
    all_to_all x1, blocking collectives, shards(): lax.all_to_all(volts[None], ('chan', 'tm'), split_axis=2, concat_axis=0,...  186 us
    ppermute x1, waiting for transfers between devices, passed_along(): return lax.ppermute(block, axis, route)  134 us
    convert_element_type x1, other arithmetic, shards(): filtered.astype(jnp.bfloat16).reshape(spectra_dev * inputs_dev, frame_len)  57.9 us
    transpose x1, local copies, waits for them, and re-layouts, shards(): jnp.transpose(all_inputs, (0, 1, 2, 4, 3, 5))  41.2 us
    another operation x1, other arithmetic  35 us
    all_gather x1, waiting for transfers between devices, shards(): lax.all_gather(slab_volts[:, :, :, None, :], 'blk', axis=3, tiled=True)  29.6 us
    all_gather x1, local copies, waits for them, and re-layouts, shards(): lax.all_gather(slab_volts[:, :, :, None, :], 'blk', axis=3, tiled=True)  28.1 us
    reshape x1, local copies, waits for them, and re-layouts, shards(): jnp.transpose(all_inputs, (0, 1, 2, 4, 3, 5))  27.4 us
  transfers between devices with their start and end apart: 2, of which 2 were waited for; matrix products, arithmetic and copies ran while one was open for 5% of the time, Pallas kernels for 0%

commit v1 on v0

--- a/solution.py
+++ b/solution.py
@@ -1,8 +1,13 @@
+import functools
 import math
 
 import jax
 import jax.numpy as jnp
+import ml_dtypes
+import numpy as np
 from jax import lax
+from jax.experimental import pallas as pl
+from jax.experimental.pallas import tpu as pltpu
 from jax.sharding import PartitionSpec as P
 
 NCH = 1024
@@ -101,10 +106,237 @@
     return jnp.stack(results, 2)
 
 
+CHUNK = 8
+ROWS = 2 * CHUNK
+
+
+def window_rows(tap_count, frame_len):
+    offset = (np.arange(tap_count * frame_len) + 0.5) / frame_len - tap_count / 2.0
+    taper = 0.5 - 0.5 * np.cos(2.0 * np.pi * (offset + tap_count / 2.0) / tap_count)
+    rows = (np.sinc(offset) * taper).reshape(tap_count, frame_len)[::-1]
+    return np.ascontiguousarray(
+        np.broadcast_to(rows[:, None, :], (tap_count, 8, frame_len)).astype(np.float32)
+    )
+
+
+def table_rows(frame_len, chan_count):
+    turn = np.arange(chan_count)[:, None] * np.arange(frame_len)[None, :] % frame_len
+    angle = np.arange(frame_len) * (2.0 * np.pi / frame_len)
+    scale = 1.0 / math.sqrt(frame_len)
+    parts = np.stack([(np.cos(angle) * scale)[turn], (-np.sin(angle) * scale)[turn]], 0)
+    return parts.astype(ml_dtypes.bfloat16)
+
+
+def voltage_kernel(first, place_ref, x_ref, w_ref, tab_ref, gain_ref, other_ref, own_ref, filt, turned):
+    step = pl.program_id(0)
+    spectra, inputs, frame_len = x_ref.shape
+
+    @pl.when(step == 0)
+    def _():
+        def tile(idx, carry):
+            row = pl.multiple_of(idx // (frame_len // 128) * 16, 16)
+            col = pl.multiple_of(idx % (frame_len // 128) * 128, 128)
+            lo = max(0, first - TAPS + 1)
+            hi = min(spectra, first + CHUNK)
+            held = {
+                s: x_ref[s, pl.ds(row, 16), pl.ds(col, 128)].astype(jnp.float32).reshape(2, 8, 128)
+                for s in range(lo, hi)
+            }
+            sums = [None] * CHUNK
+            for tap in range(TAPS):
+                weight = w_ref[tap, :, pl.ds(col, 128)]
+                for out in range(CHUNK):
+                    s = first + out - tap
+                    if lo <= s < hi:
+                        term = held[s] * weight
+                        sums[out] = term if sums[out] is None else sums[out] + term
+            for out in range(CHUNK):
+                total = sums[out]
+                if total is None:
+                    total = jnp.zeros((2, 8, 128), jnp.float32)
+                filt[pl.ds(pl.multiple_of(out * inputs + row, 16), 16), pl.ds(col, 128)] = (
+                    total.reshape(16, 128).astype(jnp.bfloat16)
+                )
+            return carry
+
+        lax.fori_loop(0, inputs // 16 * (frame_len // 128), tile, 0)
+
+    chans = tab_ref.shape[1]
+    both = lax.dot_general(
+        tab_ref[...].reshape(2 * chans, frame_len),
+        filt[...],
+        (((1,), (1,)), ((), ())),
+        preferred_element_type=jnp.float32,
+    )
+    for s in range(CHUNK):
+        real = both[:chans, s * inputs : (s + 1) * inputs]
+        imag = both[chans:, s * inputs : (s + 1) * inputs]
+        turned[s * chans : (s + 1) * chans, :] = real * gain_ref[0] - imag * gain_ref[1]
+        turned[(CHUNK + s) * chans : (CHUNK + s + 1) * chans, :] = real * gain_ref[1] + imag * gain_ref[0]
+
+    def write(out_ref):
+        def one(chan, carry):
+            out_ref[0, chan] = turned[pl.ds(chan, ROWS, stride=chans), :].astype(jnp.bfloat16)
+            return carry
+
+        lax.fori_loop(0, chans, one, 0, unroll=8)
+
+    half = pl.num_programs(0) // 2
+
+    @pl.when(step < half)
+    def _():
+        write(other_ref)
+
+    @pl.when(step >= half)
+    def _():
+        write(own_ref)
+
+
+def voltage_chunk(place, samples, window, table, gains, first):
+    spectra, inputs, frame_len = samples.shape
+    slabs = 4
+    chans = table.shape[1] // (2 * slabs)
+
+    def slab(step, place_ref):
+        part = place_ref[1] ^ (1 - step // slabs)
+        return (place_ref[0] ^ (step % slabs)) * 2 + part
+
+    out = jax.ShapeDtypeStruct((slabs, chans, ROWS, inputs), jnp.bfloat16)
+    flops = 2 * table.shape[1] * 2 * frame_len * CHUNK * inputs
+    return pl.pallas_call(
+        functools.partial(voltage_kernel, first),
+        grid_spec=pltpu.PrefetchScalarGridSpec(
+            num_scalar_prefetch=1,
+            grid=(2 * slabs,),
+            in_specs=[
+                pl.BlockSpec((spectra, inputs, frame_len), lambda g, p: (0, 0, 0), pipeline_mode=pl.Buffered(1)),
+                pl.BlockSpec((TAPS, 8, frame_len), lambda g, p: (0, 0, 0), pipeline_mode=pl.Buffered(1)),
+                pl.BlockSpec((2, chans, frame_len), lambda g, p: (0, slab(g, p), 0)),
+                pl.BlockSpec((2, chans, inputs), lambda g, p: (0, slab(g, p), 0)),
+            ],
+            out_specs=[
+                pl.BlockSpec((1, chans, ROWS, inputs), lambda g, p: (jnp.minimum(g, slabs - 1), 0, 0, 0)),
+                pl.BlockSpec((1, chans, ROWS, inputs), lambda g, p: (jnp.maximum(g - slabs, 0), 0, 0, 0)),
+            ],
+            scratch_shapes=[
+                pltpu.VMEM((CHUNK * inputs, frame_len), jnp.bfloat16),
+                pltpu.VMEM((ROWS * chans, inputs), jnp.float32),
+            ],
+        ),
+        out_shape=[out, out],
+        compiler_params=pltpu.CompilerParams(vmem_limit_bytes=40 << 20),
+        cost_estimate=pl.CostEstimate(flops=flops, bytes_accessed=24 << 20, transcendentals=0),
+    )(place, samples, window, table, gains)
+
+
+def pair_kernel(scale, parts, where_ref, *refs):
+    out_ref = refs[-1]
+    slot = pl.program_id(0)
+    sides = []
+    for side in range(2):
+        near = where_ref[slot * 4 + side * 2 + 1] == 0
+        mine = refs[side * 2 * parts : side * 2 * parts + parts]
+        far = refs[side * 2 * parts + parts : (side + 1) * 2 * parts]
+        sides.append((near, mine, far))
+
+    def one(chan, carry):
+        tiles = []
+        for near, mine, far in sides:
+            tiles.append(
+                [jnp.where(near, m[0, chan], f[0, chan]).astype(jnp.float32) for m, f in zip(mine, far)]
+            )
+        first = jnp.concatenate(tiles[0], 0).astype(jnp.bfloat16)
+        second = jnp.concatenate(tiles[1], 0).astype(jnp.bfloat16)
+        swapped = jnp.concatenate(
+            [piece for x in tiles[1] for piece in (-x[CHUNK:], x[:CHUNK])], 0
+        ).astype(jnp.bfloat16)
+        both = lax.dot_general(
+            first,
+            jnp.concatenate([second, swapped], 1),
+            (((0,), (0,)), ((), ())),
+            preferred_element_type=jnp.float32,
+        ) * scale
+        out_ref[0, chan, 0] = both[:, :BLOCK]
+        out_ref[1, chan, 0] = both[:, BLOCK:]
+        return carry
+
+    lax.fori_loop(0, out_ref.shape[1], one, 0, unroll=4)
+
+
+def pair_products(where, mine, far, slots, scale):
+    blocks, chans, rows, inputs = mine[0].shape
+    step = 16
+    parts = len(mine)
+
+    def spec(side):
+        return pl.BlockSpec((1, step, rows, inputs), lambda m, c, w: (w[m * 4 + side * 2], c, 0, 0))
+
+    return pl.pallas_call(
+        functools.partial(pair_kernel, scale, parts),
+        grid_spec=pltpu.PrefetchScalarGridSpec(
+            num_scalar_prefetch=1,
+            grid=(slots, chans // step),
+            in_specs=[spec(0)] * (2 * parts) + [spec(1)] * (2 * parts),
+            out_specs=pl.BlockSpec((2, step, 1, BLOCK, BLOCK), lambda m, c, w: (0, c, m, 0, 0)),
+        ),
+        out_shape=jax.ShapeDtypeStruct((2, chans, slots, BLOCK, BLOCK), jnp.float32),
+        compiler_params=pltpu.CompilerParams(vmem_limit_bytes=40 << 20),
+        cost_estimate=pl.CostEstimate(flops=4 << 30, bytes_accessed=50 << 20, transcendentals=0),
+    )(where, *mine, *far, *mine, *far)
+
+
+def quick_shards(samples, channel_gains, block_pairs):
+    spectra = samples.shape[0]
+    chan, part, half = lax.axis_index("chan"), lax.axis_index("tm"), lax.axis_index("blk")
+    place = jnp.stack([chan, part]).astype(jnp.int32)
+    window = jnp.asarray(window_rows(TAPS, samples.shape[2]))
+    table = jnp.asarray(table_rows(samples.shape[2], NCH))
+    early = part == 0
+
+    def made(first):
+        return voltage_chunk(place, samples, window, table, channel_gains, first)
+
+    def across(block):
+        return lax.ppermute(block, "tm", [(0, 1), (1, 0)])
+
+    def spread(pieces):
+        moved = [pieces[0]]
+        for d in range(1, 4):
+            moved.append(lax.ppermute(pieces[d], "chan", [(i, i ^ d) for i in range(4)]))
+        mine = jnp.stack(moved, 0)
+        return mine, lax.ppermute(mine, "blk", [(0, 1), (1, 0)])
+
+    def added(a, b):
+        return (a.astype(jnp.float32) + b.astype(jnp.float32)).astype(jnp.bfloat16)
+
+    mine, far = [], []
+    for chunk in range(spectra // CHUNK):
+        other, own = made(chunk * CHUNK)
+        got = across(other)
+        other_tail, own_tail = made(spectra + chunk * CHUNK)
+        got_tail = lax.ppermute(other_tail, "tm", [(0, 1)])
+        for pieces in (
+            [jnp.where(early, own[d], got[d]) for d in range(4)],
+            [
+                jnp.where(early, added(got[d], own_tail[d]), added(own[d], got_tail[d]))
+                for d in range(4)
+            ],
+        ):
+            a, b = spread(pieces)
+            mine.append(a)
+            far.append(b)
+    source = (block_pairs // 2) ^ chan
+    elsewhere = (block_pairs % 2) ^ half
+    where = jnp.stack([source, elsewhere], 2).reshape(-1).astype(jnp.int32)
+    return pair_products(where, mine, far, block_pairs.shape[0], 1.0 / math.sqrt(2 * spectra))
+
+
 def solution(mesh):
+    sizes = dict(mesh.shape)
+    quick = sizes["chan"] == 4 and sizes["tm"] == 2 and sizes["blk"] == 2
     placed = (P("tm", ("grp", "chan", "blk"), None), P(None, None, ("chan", "blk")), P("blk", None))
     return jax.shard_map(
-        shards,
+        quick_shards if quick else shards,
         mesh=mesh,
         in_specs=placed,
         out_specs=P(None, ("grp", "chan", "tm"), "blk", None, None),

time: 738 us -> 386 us (0.52)
  blocking collectives: 186 us -> 0 us
  local copies, waits for them, and re-layouts: 186 us -> 6.64 us
  Pallas kernels: 0 us -> 141 us
  other arithmetic: 143 us -> 16.4 us
  matrix products: 38.6 us -> 0 us
  starting transfers between devices: 1.28 us -> 30.1 us
  waiting for transfers between devices: 163 us -> 186 us
  between operations: 16 us -> 0.11 us
    all_to_all x1 -> x0, blocking collectives: 186 us -> none  [shards(): lax.all_to_all(volts[None], ('chan', 'tm'), split_axis=2, concat_axis=0,...]
    pallas_call x0 -> x5, Pallas kernels: none -> 141 us  [the longest x4 115 us: voltage_chunk(): pl.pallas_call(functools.partial(voltage_kernel, first), grid_spec=pltpu....]
    convert_element_type x1 -> x0, other arithmetic: 57.9 us -> none  [shards(): filtered.astype(jnp.bfloat16).reshape(spectra_dev * inputs_dev, frame_len)]
    another operation x4 -> x7, other arithmetic: 62 us -> 5.21 us  [the longest x4 5.12 us: spread(): mine = jnp.stack(moved, 0)]
    transpose x2 -> x0, local copies, waits for them, and re-layouts: 55.2 us -> none  [the longest x1 41.2 us: shards(): jnp.transpose(all_inputs, (0, 1, 2, 4, 3, 5))]
    ppermute x1 -> x20, waiting for transfers between devices: 134 us -> 186 us  [the longest x12 112 us: spread(): lax.ppermute(pieces[d], 'chan', [(i, i ^ d) for i in range(4)])]
    dot_general x5 -> x0, matrix products: 38.6 us -> none  [the longest x1 21.4 us: shards(): lax.dot_general(dft_table, filtered, (((1,), (1,)), ((), ())), preferred_...]
    all_gather x1 -> x0, waiting for transfers between devices: 29.6 us -> none  [shards(): lax.all_gather(slab_volts[:, :, :, None, :], 'blk', axis=3, tiled=True)]
  transfers between devices with their start and end apart: 2 -> 20, of which waited for: 2 -> 9; matrix products, arithmetic and copies ran while one was open for 5% -> 4% of each run, Pallas kernels for 0% -> 23%
where the time goes in v1:
time: 386 us; the launch traced here: 381 us
  waiting for transfers between devices  186 us (48%)
  Pallas kernels  141 us (37%)
  starting transfers between devices  30.1 us (8%)
  other arithmetic  16.4 us (4%)
  local copies, waits for them, and re-layouts  6.64 us (2%)
    pallas_call x4, Pallas kernels, voltage_chunk(): pl.pallas_call(functools.partial(voltage_kernel, first), grid_spec=pltpu....  115 us
    ppermute x12, waiting for transfers between devices, spread(): lax.ppermute(pieces[d], 'chan', [(i, i ^ d) for i in range(4)])  112 us
    ppermute x2, waiting for transfers between devices, across(): return lax.ppermute(block, 'tm', [(0, 1), (1, 0)])  43.6 us
    ppermute x2, waiting for transfers between devices, quick_shards(): got_tail = lax.ppermute(other_tail, 'tm', [(0, 1)])  27.3 us
    pallas_call x1, Pallas kernels, pair_products(): pl.pallas_call(functools.partial(pair_kernel, scale, parts), grid_spec=pl...  26.1 us
    ppermute x12, starting transfers between devices, spread(): lax.ppermute(pieces[d], 'chan', [(i, i ^ d) for i in range(4)])  15.2 us
    select_n x2, other arithmetic, quick_shards(): jnp.where(early, added(got[d], own_tail[d]), added(own[d], got_tail[d]))  7.97 us
  transfers between devices with their start and end apart: 20, of which 9 were waited for; matrix products, arithmetic and copies ran while one was open for 4% of the time, Pallas kernels for 23%

profile of v1, /device:TPU:19, one launch (start us, length us, event | category | flops | bytes accessed | tf_op | source)
XLA Modules:
  0.0 380.9 jit_solution(4040638698605874209)
XLA Ops:
  0.0 0.1 pad_add_fusion.1.place_ref
  0.1 1.2 copy-done.5
  1.3 1.2 copy-done.6
  2.5 25.8 %shard_map.58 = (bf16[4,128,16,128]{3,2,1,0:T(8,128)(2,1)}, bf16[4,128,16,128]{3,2,1,0:T(8,128)(2,1)S(1)}) custom-call(s32[2]{0:T(128)S(1)} %pad_add_fusion.1.place_ref, bf16[16,128,2048]{2,1,0:T(8,128)(2,1)} %x_ref.7, f32[16,8,2048]{2,1,0:T(8,128)S(1)} %copy-done.6, bf16[2,1024,2048]{2,1,0:T(8,128)(2,1)} %constant.43.clone.tab_ref, ...), custom_call_target="tpu_custom_call" | custom-call | flops 8589934592 | bytes 25165824 | tf_op jit(solution)/shard_map/pallas_call | solution.py:206
  28.3 1.3 copy-done.4
  29.7 1.3 collective-permute-start.12
  30.9 31.6 %shard_map.57 = (bf16[4,128,16,128]{3,2,1,0:T(8,128)(2,1)}, bf16[4,128,16,128]{3,2,1,0:T(8,128)(2,1)S(1)}) custom-call(s32[2]{0:T(128)S(1)} %pad_add_fusion.1.place_ref, bf16[16,128,2048]{2,1,0:T(8,128)(2,1)} %x_ref.7, f32[16,8,2048]{2,1,0:T(8,128)S(1)} %copy-done.6, bf16[2,1024,2048]{2,1,0:T(8,128)(2,1)} %constant.43.clone.tab_ref, ...), custom_call_target="tpu_custom_call" | custom-call | flops 8589934592 | bytes 25165824 | tf_op jit(solution)/shard_map/pallas_call | solution.py:206
  62.6 1.3 copy-done
  63.9 3.4 collective-permute-start.8
  67.3 31.4 %shard_map.56 = (bf16[4,128,16,128]{3,2,1,0:T(8,128)(2,1)}, bf16[4,128,16,128]{3,2,1,0:T(8,128)(2,1)S(1)}) custom-call(s32[2]{0:T(128)S(1)} %pad_add_fusion.1.place_ref, bf16[16,128,2048]{2,1,0:T(8,128)(2,1)} %x_ref.7, f32[16,8,2048]{2,1,0:T(8,128)S(1)} %copy-done.6, bf16[2,1024,2048]{2,1,0:T(8,128)(2,1)} %constant.43.clone.tab_ref, ...), custom_call_target="tpu_custom_call" | custom-call | flops 8589934592 | bytes 25165824 | tf_op jit(solution)/shard_map/pallas_call | solution.py:206
  98.7 1.4 copy-done.2
  100.0 1.3 collective-permute-start.4
  101.3 0.0 copy-done.7
  101.3 26.3 %shard_map.55 = (bf16[4,128,16,128]{3,2,1,0:T(8,128)(2,1)}, bf16[4,128,16,128]{3,2,1,0:T(8,128)(2,1)S(1)}) custom-call(s32[2]{0:T(128)S(1)} %pad_add_fusion.1.place_ref, bf16[16,128,2048]{2,1,0:T(8,128)(2,1)} %x_ref.7, f32[16,8,2048]{2,1,0:T(8,128)S(1)} %copy-done.7, bf16[2,1024,2048]{2,1,0:T(8,128)(2,1)} %constant.43.clone.tab_ref, ...), custom_call_target="tpu_custom_call" | custom-call | flops 8589934592 | bytes 25165824 | tf_op jit(solution)/shard_map/pallas_call | solution.py:206
  127.7 3.4 collective-permute-start
  131.1 0.0 collective-permute-done.12
  131.1 0.0 collective-permute-done.8
  131.1 4.7 %fusion.7 = (bf16[1,128,16,128]{3,2,1,0:T(8,128)(2,1)S(1)}, bf16[128,16,128]{2,1,0:T(8,128)(2,1)S(1)}, bf16[128,16,128]{2,1,0:T(8,128)(2,1)S(1)}, bf16[128,16,12...) fusion(bf16[4,128,16,128]{3,2,1,0:T(8,128)(2,1)} %collective-permute-done.12, bf16[4,128,16,128]{3,2,1,0:T(8,128)(2,1)} %copy-done.4, ...), kind=kLoop, calls=%fused_computation.27 | loop fusion | flops 9699328 | bytes 11010049 | tf_op jit(solution)/shard_map/jit(_where)/select_n | solution.py:321
  135.8 0.2 collective-permute-start.15
  136.0 3.2 collective-permute-start.14
  139.2 0.0 collective-permute-start.13
  139.2 0.0 copy-done.1
  139.2 1.7 select_bitcast_fusion.2
  141.0 27.3 %collective-permute-done.4 = bf16[4,128,16,128]{3,2,1,0:T(8,128)(2,1)} collective-permute-done((bf16[4,128,16,128]{3,2,1,0:T(8,128)(2,1)}, bf16[4,128,16,128]{3,2,1,0:T(8,128)(2,1)}, u32[]{:S(2)}, u32[]{:S(2)}) %collective-permute-start.4) | collective-permute-done | bytes 2097184 | tf_op jit(solution)/shard_map/ppermute | solution.py:317
  168.2 1.3 collective-permute-start.9
  169.5 43.6 %collective-permute-done = bf16[4,128,16,128]{3,2,1,0:T(8,128)(2,1)} collective-permute-done((bf16[4,128,16,128]{3,2,1,0:T(8,128)(2,1)}, bf16[4,128,16,128]{3,2,1,0:T(8,128)(2,1)}, u32[]{:S(2)}, u32[]{:S(2)}) %collective-permute-start) | collective-permute-done | bytes 2097184 | tf_op jit(solution)/shard_map/ppermute | solution.py:300
  213.2 0.1 collective-permute-start.10
  213.2 0.0 copy-done.3
  213.2 3.3 fusion
  216.5 0.0 collective-permute-done.15
  216.6 2.5 collective-permute-start.11
  219.0 0.0 collective-permute-done.14
  219.0 1.1 collective-permute-start.1
  220.1 1.5 broadcast_select_fusion.1
  221.6 0.0 collective-permute-done.13
  221.6 0.3 collective-permute-start.2
  221.9 0.0 collective-permute-done.9
  221.9 1.4 collective-permute-start.3
  223.3 23.0 %collective-permute-done.10 = bf16[128,16,128]{2,1,0:T(8,128)(2,1)S(1)} collective-permute-done((bf16[128,16,128]{2,1,0:T(8,128)(2,1)S(1)}, bf16[128,16,128]{2,1,0:T(8,128)(2,1)S(1)}, u32[]{:S(2)}, u32[]{:S(2)}) %collective-permute-start.10) | collective-permute-done | bytes 524320 | tf_op jit(solution)/shard_map/ppermute | solution.py:305
  246.3 4.8 %collective-permute-start.7 = (bf16[128,16,128]{2,1,0:T(8,128)(2,1)S(1)}, bf16[128,16,128]{2,1,0:T(8,128)(2,1)S(1)}, u32[]{:S(2)}, u32[]{:S(2)}) collective-permute-start(bf16[128,16,128]{2,1,0:T(8,128)(2,1)S(1)} %get-tuple-element.26), channel_id=1, source_target_pairs={{0,12},{4,8},{8,4},{12,0},{1,13},{5,9},{9,5},{13,1},{2,14},{6,10},... | collective-permute-start | bytes 1572872 | tf_op jit(solution)/shard_map/ppermute | solution.py:305
  251.1 44.3 %collective-permute-done.11 = bf16[128,16,128]{2,1,0:T(8,128)(2,1)S(1)} collective-permute-done((bf16[128,16,128]{2,1,0:T(8,128)(2,1)S(1)}, bf16[128,16,128]{2,1,0:T(8,128)(2,1)S(1)}, u32[]{:S(2)}, u32[]{:S(2)}) %collective-permute-start.11) | collective-permute-done | bytes 524320 | tf_op jit(solution)/shard_map/ppermute | solution.py:305
  295.4 0.0 collective-permute-start.6
  295.4 0.0 collective-permute-done.1
  295.4 0.4 collective-permute-start.5
  295.8 0.3 pad_maximum_fusion.3.refs_3_.refs_11_
  296.1 1.6 pad_maximum_fusion.2.refs_2_.refs_10_
  297.7 16.0 %collective-permute-done.2 = bf16[128,16,128]{2,1,0:T(8,128)(2,1)S(1)} collective-permute-done((bf16[128,16,128]{2,1,0:T(8,128)(2,1)S(1)}, bf16[128,16,128]{2,1,0:T(8,128)(2,1)S(1)}, u32[]{:S(2)}, u32[]{:S(2)}) %collective-permute-start.2) | collective-permute-done | bytes 524320 | tf_op jit(solution)/shard_map/ppermute | solution.py:305
  313.8 2.7 collective-permute-start.18
  316.5 12.6 %collective-permute-done.3 = bf16[128,16,128]{2,1,0:T(8,128)(2,1)S(1)} collective-permute-done((bf16[128,16,128]{2,1,0:T(8,128)(2,1)S(1)}, bf16[128,16,128]{2,1,0:T(8,128)(2,1)S(1)}, u32[]{:S(2)}, u32[]{:S(2)}) %collective-permute-start.3) | collective-permute-done | bytes 524320 | tf_op jit(solution)/shard_map/ppermute | solution.py:305
  329.1 0.6 collective-permute-start.19
  329.7 1.6 pad_maximum_fusion.refs_0_.refs_8_
  331.3 9.0 %collective-permute-done.7 = bf16[128,16,128]{2,1,0:T(8,128)(2,1)S(1)} collective-permute-done((bf16[128,16,128]{2,1,0:T(8,128)(2,1)S(1)}, bf16[128,16,128]{2,1,0:T(8,128)(2,1)S(1)}, u32[]{:S(2)}, u32[]{:S(2)}) %collective-permute-start.7) | collective-permute-done | bytes 524320 | tf_op jit(solution)/shard_map/ppermute | solution.py:305
  340.3 0.6 collective-permute-start.16
  340.9 6.6 %collective-permute-done.6 = bf16[128,16,128]{2,1,0:T(8,128)(2,1)S(1)} collective-permute-done((bf16[128,16,128]{2,1,0:T(8,128)(2,1)S(1)}, bf16[128,16,128]{2,1,0:T(8,128)(2,1)S(1)}, u32[]{:S(2)}, u32[]{:S(2)}) %collective-permute-start.6) | collective-permute-done | bytes 524320 | tf_op jit(solution)/shard_map/ppermute | solution.py:305
  347.5 0.0 collective-permute-done.5
  347.5 1.6 pad_maximum_fusion.1.refs_1_.refs_9_
  349.1 1.6 collective-permute-start.17
  350.7 0.1 copy.6
  350.8 0.1 reshape.75.where_ref
  350.9 0.0 collective-permute-done.18.refs_6_.refs_14_
  350.9 0.0 collective-permute-done.19.refs_7_.refs_15_
  350.9 0.0 collective-permute-done.16.refs_4_.refs_12_
  350.9 3.9 %collective-permute-done.17.refs_5_.refs_13_ = bf16[4,128,16,128]{3,2,1,0:T(8,128)(2,1)} collective-permute-done((bf16[4,128,16,128]{3,2,1,0:T(8,128)(2,1)}, bf16[4,128,16,128]{3,2,1,0:T(8,128)(2,1)}, u32[]{:S(2)}, u32[]{:S(2)}) %collective-permute-start.17) | collective-permute-done | bytes 2097184 | tf_op jit(solution)/shard_map/ppermute | solution.py:307
  354.8 26.1 %shard_map.59 = f32[2,128,2,128,128]{4,3,2,1,0:T(8,128)} custom-call(s32[8]{0:T(128)S(1)} %reshape.75.where_ref, bf16[4,128,16,128]{3,2,1,0:T(8,128)(2,1)} %pad_maximum_fusion.refs_0_.refs_8_, bf16[4,128,16,128]{3,2,1,0:T(8,128)(2,1)} %pad_maximum_fusion.1.refs_1_.refs_9_, bf16[4,128,16,128]{3,2,1,0:T(8,128)(2,1)} %pad_maximum_fusion.2.refs_2_.refs_10_, ...), custom_call_target="tpu_custom_call" | custom-call | flops 4294967296 | bytes 52428800 | tf_op jit(solution)/shard_map/pallas_call | solution.py:274
  (12 shorter events, 0.0 us)
Async XLA Ops:
  0.1 1.2 copy-start.5
  1.3 1.2 copy-start.6
  28.3 1.3 copy-start.4
  29.7 101.4 %collective-permute-start.12 = (bf16[4,128,16,128]{3,2,1,0:T(8,128)(2,1)}, bf16[4,128,16,128]{3,2,1,0:T(8,128)(2,1)}, u32[]{:S(2)}, u32[]{:S(2)}) collective-permute-start(bf16[4,128,16,128]{3,2,1,0:T(8,128)(2,1)} %get-tuple-element.20), channel_id=1, source_target_pairs={{0,2},{1,3},{4,6},{5,7},{8,10},{9,11},{12,14},{13,15},{16,18},{17,... | collective-permute-start | bytes 6291464 | tf_op jit(solution)/shard_map/ppermute | solution.py:317
  62.6 1.3 copy-start
  63.9 37.5 %copy-start.7 = (f32[16,8,2048]{2,1,0:T(8,128)S(1)}, f32[16,8,2048]{2,1,0:T(8,128)}, u32[]{:S(2)}) copy-start(f32[16,8,2048]{2,1,0:T(8,128)} %constant.42.clone.w_ref) | copy-start | bytes 3145732
  63.9 67.2 %collective-permute-start.8 = (bf16[4,128,16,128]{3,2,1,0:T(8,128)(2,1)}, bf16[4,128,16,128]{3,2,1,0:T(8,128)(2,1)}, u32[]{:S(2)}, u32[]{:S(2)}) collective-permute-start(bf16[4,128,16,128]{3,2,1,0:T(8,128)(2,1)} %get-tuple-element.18), channel_id=1, source_target_pairs={{0,2},{2,0},{1,3},{3,1},{4,6},{6,4},{5,7},{7,5},{8,10},{10,8},{9,1... | collective-permute-start | bytes 6291464 | tf_op jit(solution)/shard_map/ppermute | solution.py:300
  98.7 1.4 copy-start.2
  100.0 68.2 %collective-permute-start.4 = (bf16[4,128,16,128]{3,2,1,0:T(8,128)(2,1)}, bf16[4,128,16,128]{3,2,1,0:T(8,128)(2,1)}, u32[]{:S(2)}, u32[]{:S(2)}) collective-permute-start(bf16[4,128,16,128]{3,2,1,0:T(8,128)(2,1)} %get-tuple-element.16), channel_id=1, source_target_pairs={{0,2},{1,3},{4,6},{5,7},{8,10},{9,11},{12,14},{13,15},{16,18},{17,... | collective-permute-start | bytes 6291464 | tf_op jit(solution)/shard_map/ppermute | solution.py:317
  127.7 85.5 %collective-permute-start = (bf16[4,128,16,128]{3,2,1,0:T(8,128)(2,1)}, bf16[4,128,16,128]{3,2,1,0:T(8,128)(2,1)}, u32[]{:S(2)}, u32[]{:S(2)}) collective-permute-start(bf16[4,128,16,128]{3,2,1,0:T(8,128)(2,1)} %get-tuple-element.14), channel_id=1, source_target_pairs={{0,2},{2,0},{1,3},{3,1},{4,6},{6,4},{5,7},{7,5},{8,10},{10,8},{9,1... | collective-permute-start | bytes 6291464 | tf_op jit(solution)/shard_map/ppermute | solution.py:300
  131.1 8.1 %copy-start.1 = (bf16[4,128,16,128]{3,2,1,0:T(8,128)(2,1)S(1)}, bf16[4,128,16,128]{3,2,1,0:T(8,128)(2,1)}, u32[]{:S(2)}) copy-start(bf16[4,128,16,128]{3,2,1,0:T(8,128)(2,1)} %copy-done) | copy-start | bytes 6291460
  135.8 80.8 %collective-permute-start.15 = (bf16[128,16,128]{2,1,0:T(8,128)(2,1)S(1)}, bf16[128,16,128]{2,1,0:T(8,128)(2,1)S(1)}, u32[]{:S(2)}, u32[]{:S(2)}) collective-permute-start(bf16[128,16,128]{2,1,0:T(8,128)(2,1)S(1)} %get-tuple-element.22), channel_id=1, source_target_pairs={{0,12},{4,8},{8,4},{12,0},{1,13},{5,9},{9,5},{13,1},{2,14},{6,10},... | collective-permute-start | bytes 1572872 | tf_op jit(solution)/shard_map/ppermute | solution.py:305
  136.0 83.0 %collective-permute-start.14 = (bf16[128,16,128]{2,1,0:T(8,128)(2,1)S(1)}, bf16[128,16,128]{2,1,0:T(8,128)(2,1)S(1)}, u32[]{:S(2)}, u32[]{:S(2)}) collective-permute-start(bf16[128,16,128]{2,1,0:T(8,128)(2,1)S(1)} %get-tuple-element.23), channel_id=1, source_target_pairs={{0,8},{4,12},{8,0},{12,4},{1,9},{5,13},{9,1},{13,5},{2,10},{6,14},... | collective-permute-start | bytes 1572872 | tf_op jit(solution)/shard_map/ppermute | solution.py:305
  139.2 74.0 %copy-start.3 = (bf16[4,128,16,128]{3,2,1,0:T(8,128)(2,1)S(1)}, bf16[4,128,16,128]{3,2,1,0:T(8,128)(2,1)}, u32[]{:S(2)}) copy-start(bf16[4,128,16,128]{3,2,1,0:T(8,128)(2,1)} %copy-done.2) | copy-start | bytes 6291460
  139.2 82.4 %collective-permute-start.13 = (bf16[128,16,128]{2,1,0:T(8,128)(2,1)S(1)}, bf16[128,16,128]{2,1,0:T(8,128)(2,1)S(1)}, u32[]{:S(2)}, u32[]{:S(2)}) collective-permute-start(bf16[128,16,128]{2,1,0:T(8,128)(2,1)S(1)} %get-tuple-element.24), channel_id=1, source_target_pairs={{0,4},{4,0},{8,12},{12,8},{1,5},{5,1},{9,13},{13,9},{2,6},{6,2},{1... | collective-permute-start | bytes 1572872 | tf_op jit(solution)/shard_map/ppermute | solution.py:305
  168.2 53.7 %collective-permute-start.9 = (bf16[128,16,128]{2,1,0:T(8,128)(2,1)S(1)}, bf16[128,16,128]{2,1,0:T(8,128)(2,1)S(1)}, u32[]{:S(2)}, u32[]{:S(2)}) collective-permute-start(bf16[128,16,128]{2,1,0:T(8,128)(2,1)S(1)} %get-tuple-element.30), channel_id=1, source_target_pairs={{0,4},{4,0},{8,12},{12,8},{1,5},{5,1},{9,13},{13,9},{2,6},{6,2},{1... | collective-permute-start | bytes 1572872 | tf_op jit(solution)/shard_map/ppermute | solution.py:305
  213.2 33.1 %collective-permute-start.10 = (bf16[128,16,128]{2,1,0:T(8,128)(2,1)S(1)}, bf16[128,16,128]{2,1,0:T(8,128)(2,1)S(1)}, u32[]{:S(2)}, u32[]{:S(2)}) collective-permute-start(bf16[128,16,128]{2,1,0:T(8,128)(2,1)S(1)} %get-tuple-element.31), channel_id=1, source_target_pairs={{0,8},{4,12},{8,0},{12,4},{1,9},{5,13},{9,1},{13,5},{2,10},{6,14},... | collective-permute-start | bytes 1572872 | tf_op jit(solution)/shard_map/ppermute | solution.py:305
  216.6 78.8 %collective-permute-start.11 = (bf16[128,16,128]{2,1,0:T(8,128)(2,1)S(1)}, bf16[128,16,128]{2,1,0:T(8,128)(2,1)S(1)}, u32[]{:S(2)}, u32[]{:S(2)}) collective-permute-start(bf16[128,16,128]{2,1,0:T(8,128)(2,1)S(1)} %get-tuple-element.32), channel_id=1, source_target_pairs={{0,12},{4,8},{8,4},{12,0},{1,13},{5,9},{9,5},{13,1},{2,14},{6,10},... | collective-permute-start | bytes 1572872 | tf_op jit(solution)/shard_map/ppermute | solution.py:305
  219.0 76.3 %collective-permute-start.1 = (bf16[128,16,128]{2,1,0:T(8,128)(2,1)S(1)}, bf16[128,16,128]{2,1,0:T(8,128)(2,1)S(1)}, u32[]{:S(2)}, u32[]{:S(2)}) collective-permute-start(bf16[128,16,128]{2,1,0:T(8,128)(2,1)S(1)} %get-tuple-element.33), channel_id=1, source_target_pairs={{0,4},{4,0},{8,12},{12,8},{1,5},{5,1},{9,13},{13,9},{2,6},{6,2},{1... | collective-permute-start | bytes 1572872 | tf_op jit(solution)/shard_map/ppermute | solution.py:305
  221.6 92.1 %collective-permute-start.2 = (bf16[128,16,128]{2,1,0:T(8,128)(2,1)S(1)}, bf16[128,16,128]{2,1,0:T(8,128)(2,1)S(1)}, u32[]{:S(2)}, u32[]{:S(2)}) collective-permute-start(bf16[128,16,128]{2,1,0:T(8,128)(2,1)S(1)} %get-tuple-element.35), channel_id=1, source_target_pairs={{0,8},{4,12},{8,0},{12,4},{1,9},{5,13},{9,1},{13,5},{2,10},{6,14},... | collective-permute-start | bytes 1572872 | tf_op jit(solution)/shard_map/ppermute | solution.py:305
  221.9 107.2 %collective-permute-start.3 = (bf16[128,16,128]{2,1,0:T(8,128)(2,1)S(1)}, bf16[128,16,128]{2,1,0:T(8,128)(2,1)S(1)}, u32[]{:S(2)}, u32[]{:S(2)}) collective-permute-start(bf16[128,16,128]{2,1,0:T(8,128)(2,1)S(1)} %get-tuple-element.36), channel_id=1, source_target_pairs={{0,12},{4,8},{8,4},{12,0},{1,13},{5,9},{9,5},{13,1},{2,14},{6,10},... | collective-permute-start | bytes 1572872 | tf_op jit(solution)/shard_map/ppermute | solution.py:305
  246.3 94.0 %collective-permute-start.7 = (bf16[128,16,128]{2,1,0:T(8,128)(2,1)S(1)}, bf16[128,16,128]{2,1,0:T(8,128)(2,1)S(1)}, u32[]{:S(2)}, u32[]{:S(2)}) collective-permute-start(bf16[128,16,128]{2,1,0:T(8,128)(2,1)S(1)} %get-tuple-element.26), channel_id=1, source_target_pairs={{0,12},{4,8},{8,4},{12,0},{1,13},{5,9},{9,5},{13,1},{2,14},{6,10},... | collective-permute-start | bytes 1572872 | tf_op jit(solution)/shard_map/ppermute | solution.py:305
  295.4 52.1 %collective-permute-start.6 = (bf16[128,16,128]{2,1,0:T(8,128)(2,1)S(1)}, bf16[128,16,128]{2,1,0:T(8,128)(2,1)S(1)}, u32[]{:S(2)}, u32[]{:S(2)}) collective-permute-start(bf16[128,16,128]{2,1,0:T(8,128)(2,1)S(1)} %get-tuple-element.27), channel_id=1, source_target_pairs={{0,8},{4,12},{8,0},{12,4},{1,9},{5,13},{9,1},{13,5},{2,10},{6,14},... | collective-permute-start | bytes 1572872 | tf_op jit(solution)/shard_map/ppermute | solution.py:305
  295.4 52.1 %collective-permute-start.5 = (bf16[128,16,128]{2,1,0:T(8,128)(2,1)S(1)}, bf16[128,16,128]{2,1,0:T(8,128)(2,1)S(1)}, u32[]{:S(2)}, u32[]{:S(2)}) collective-permute-start(bf16[128,16,128]{2,1,0:T(8,128)(2,1)S(1)} %get-tuple-element.28), channel_id=1, source_target_pairs={{0,4},{4,0},{8,12},{12,8},{1,5},{5,1},{9,13},{13,9},{2,6},{6,2},{1... | collective-permute-start | bytes 1572872 | tf_op jit(solution)/shard_map/ppermute | solution.py:305
  313.8 37.1 %collective-permute-start.18 = (bf16[4,128,16,128]{3,2,1,0:T(8,128)(2,1)}, bf16[4,128,16,128]{3,2,1,0:T(8,128)(2,1)}, u32[]{:S(2)}, u32[]{:S(2)}) collective-permute-start(bf16[4,128,16,128]{3,2,1,0:T(8,128)(2,1)} %pad_maximum_fusion.2.refs_2_.refs_10_), channel_id=1, source_target_pairs={{0,1},{1,0},{2,3},{3,2},{4,5},{5,4},{6,7},{7,6},{8,9},{9,8},{10,11... | collective-permute-start | bytes 6291464 | tf_op jit(solution)/shard_map/ppermute | solution.py:307
  329.1 21.8 %collective-permute-start.19 = (bf16[4,128,16,128]{3,2,1,0:T(8,128)(2,1)S(1)}, bf16[4,128,16,128]{3,2,1,0:T(8,128)(2,1)}, u32[]{:S(2)}, u32[]{:S(2)}) collective-permute-start(bf16[4,128,16,128]{3,2,1,0:T(8,128)(2,1)S(1)} %pad_maximum_fusion.3.refs_3_.refs_11_), channel_id=1, source_target_pairs={{0,1},{1,0},{2,3},{3,2},{4,5},{5,4},{6,7},{7,6},{8,9},{9,8},{10,11... | collective-permute-start | bytes 6291464 | tf_op jit(solution)/shard_map/ppermute | solution.py:307
  340.3 10.6 %collective-permute-start.16 = (bf16[4,128,16,128]{3,2,1,0:T(8,128)(2,1)}, bf16[4,128,16,128]{3,2,1,0:T(8,128)(2,1)}, u32[]{:S(2)}, u32[]{:S(2)}) collective-permute-start(bf16[4,128,16,128]{3,2,1,0:T(8,128)(2,1)} %pad_maximum_fusion.refs_0_.refs_8_), channel_id=1, source_target_pairs={{0,1},{1,0},{2,3},{3,2},{4,5},{5,4},{6,7},{7,6},{8,9},{9,8},{10,11... | collective-permute-start | bytes 6291464 | tf_op jit(solution)/shard_map/ppermute | solution.py:307
  347.5 3.2 copy-start.8
  349.1 5.7 %collective-permute-start.17 = (bf16[4,128,16,128]{3,2,1,0:T(8,128)(2,1)}, bf16[4,128,16,128]{3,2,1,0:T(8,128)(2,1)}, u32[]{:S(2)}, u32[]{:S(2)}) collective-permute-start(bf16[4,128,16,128]{3,2,1,0:T(8,128)(2,1)} %pad_maximum_fusion.1.refs_1_.refs_9_), channel_id=1, source_target_pairs={{0,1},{1,0},{2,3},{3,2},{4,5},{5,4},{6,7},{7,6},{8,9},{9,8},{10,11... | collective-permute-start | bytes 6291464 | tf_op jit(solution)/shard_map/ppermute | solution.py:307

commit v2 on v1

--- a/solution.py
+++ b/solution.py
@@ -127,106 +127,112 @@
     return parts.astype(ml_dtypes.bfloat16)
 
 
-def voltage_kernel(first, place_ref, x_ref, w_ref, tab_ref, gain_ref, other_ref, own_ref, filt, turned):
+def voltage_kernel(first, place_ref, x_ref, w_ref, tab_ref, gain_ref, *refs):
+    filt, turned = refs[-2:]
+    slabs = (len(refs) - 2) // 2
     step = pl.program_id(0)
     spectra, inputs, frame_len = x_ref.shape
 
     @pl.when(step == 0)
     def _():
         def tile(idx, carry):
-            row = pl.multiple_of(idx // (frame_len // 128) * 16, 16)
-            col = pl.multiple_of(idx % (frame_len // 128) * 128, 128)
+            col = pl.multiple_of(idx * 128, 128)
+
             lo = max(0, first - TAPS + 1)
             hi = min(spectra, first + CHUNK)
-            held = {
-                s: x_ref[s, pl.ds(row, 16), pl.ds(col, 128)].astype(jnp.float32).reshape(2, 8, 128)
-                for s in range(lo, hi)
-            }
-            sums = [None] * CHUNK
-            for tap in range(TAPS):
-                weight = w_ref[tap, :, pl.ds(col, 128)]
+            weights = {}
+            rows = [[] for _ in range(CHUNK)]
+            for row in range(0, inputs, 16):
+                held = {
+                    s: x_ref[s, pl.ds(row, 16), pl.ds(col, 128)].astype(jnp.float32).reshape(2, 8, 128)
+                    for s in range(lo, hi)
+                }
+                sums = [None] * CHUNK
+                for tap in range(TAPS):
+                    if not any(lo <= first + out - tap < hi for out in range(CHUNK)):
+                        continue
+                    weight = w_ref[tap, :, pl.ds(col, 128)]
+                    for out in range(CHUNK):
+                        s = first + out - tap
+                        if lo <= s < hi:
+                            term = held[s] * weight
+                            sums[out] = term if sums[out] is None else sums[out] + term
                 for out in range(CHUNK):
-                    s = first + out - tap
-                    if lo <= s < hi:
-                        term = held[s] * weight
-                        sums[out] = term if sums[out] is None else sums[out] + term
+                    total = sums[out]
+                    if total is None:
+                        total = jnp.zeros((2, 8, 128), jnp.float32)
+                    rows[out].append(total.reshape(16, 128).astype(jnp.bfloat16))
             for out in range(CHUNK):
-                total = sums[out]
-                if total is None:
-                    total = jnp.zeros((2, 8, 128), jnp.float32)
-                filt[pl.ds(pl.multiple_of(out * inputs + row, 16), 16), pl.ds(col, 128)] = (
-                    total.reshape(16, 128).astype(jnp.bfloat16)
-                )
+                filt[pl.ds(col, 128), out * inputs : (out + 1) * inputs] = jnp.concatenate(rows[out], 0).T
             return carry
 
-        lax.fori_loop(0, inputs // 16 * (frame_len // 128), tile, 0)
-
-    chans = tab_ref.shape[1]
-    both = lax.dot_general(
-        tab_ref[...].reshape(2 * chans, frame_len),
-        filt[...],
-        (((1,), (1,)), ((), ())),
-        preferred_element_type=jnp.float32,
-    )
-    for s in range(CHUNK):
-        real = both[:chans, s * inputs : (s + 1) * inputs]
-        imag = both[chans:, s * inputs : (s + 1) * inputs]
-        turned[s * chans : (s + 1) * chans, :] = real * gain_ref[0] - imag * gain_ref[1]
-        turned[(CHUNK + s) * chans : (CHUNK + s + 1) * chans, :] = real * gain_ref[1] + imag * gain_ref[0]
-
-    def write(out_ref):
-        def one(chan, carry):
-            out_ref[0, chan] = turned[pl.ds(chan, ROWS, stride=chans), :].astype(jnp.bfloat16)
-            return carry
-
-        lax.fori_loop(0, chans, one, 0, unroll=8)
-
-    half = pl.num_programs(0) // 2
-
-    @pl.when(step < half)
-    def _():
-        write(other_ref)
-
-    @pl.when(step >= half)
-    def _():
-        write(own_ref)
+        lax.fori_loop(0, frame_len // 128, tile, 0)
+
+    both_chans = tab_ref.shape[1]
+    chans = both_chans // 2
+    width = filt.shape[1] // 4
+    each = width // inputs
+    for quarter in range(4):
+        both = jnp.dot(
+            tab_ref[...].reshape(2 * both_chans, frame_len),
+            filt[:, quarter * width : (quarter + 1) * width],
+            preferred_element_type=jnp.float32,
+        )
+        for k in range(each):
+            s = quarter * each + k
+            real = both[:both_chans, k * inputs : (k + 1) * inputs]
+            imag = both[both_chans:, k * inputs : (k + 1) * inputs]
+            low = s * PITCH
+            turned[low : low + both_chans, :] = real * gain_ref[0] - imag * gain_ref[1]
+            low = (CHUNK + s) * PITCH
+            turned[low : low + both_chans, :] = real * gain_ref[1] + imag * gain_ref[0]
+
+    part = place_ref[1]
+    for slab in range(slabs):
+
+        @pl.when(step == slab)
+        def _():
+            for out_ref, base in ((refs[slab], (1 - part) * chans), (refs[slabs + slab], part * chans)):
+
+                def one(chan, carry):
+                    out_ref[chan] = turned[pl.ds(base + chan, ROWS, stride=PITCH), :].astype(jnp.bfloat16)
+                    return carry
+
+                lax.fori_loop(0, chans, one, 0, unroll=16)
+
+
+PITCH = 257
 
 
 def voltage_chunk(place, samples, window, table, gains, first):
     spectra, inputs, frame_len = samples.shape
     slabs = 4
-    chans = table.shape[1] // (2 * slabs)
-
-    def slab(step, place_ref):
-        part = place_ref[1] ^ (1 - step // slabs)
-        return (place_ref[0] ^ (step % slabs)) * 2 + part
-
-    out = jax.ShapeDtypeStruct((slabs, chans, ROWS, inputs), jnp.bfloat16)
+    both_chans = table.shape[1] // slabs
+    out = jax.ShapeDtypeStruct((both_chans // 2, ROWS, inputs), jnp.bfloat16)
     flops = 2 * table.shape[1] * 2 * frame_len * CHUNK * inputs
-    return pl.pallas_call(
+    whole = pl.BlockSpec(out.shape, lambda g, p: (0, 0, 0))
+    outs = pl.pallas_call(
         functools.partial(voltage_kernel, first),
         grid_spec=pltpu.PrefetchScalarGridSpec(
             num_scalar_prefetch=1,
-            grid=(2 * slabs,),
+            grid=(slabs,),
             in_specs=[
                 pl.BlockSpec((spectra, inputs, frame_len), lambda g, p: (0, 0, 0), pipeline_mode=pl.Buffered(1)),
                 pl.BlockSpec((TAPS, 8, frame_len), lambda g, p: (0, 0, 0), pipeline_mode=pl.Buffered(1)),
-                pl.BlockSpec((2, chans, frame_len), lambda g, p: (0, slab(g, p), 0)),
-                pl.BlockSpec((2, chans, inputs), lambda g, p: (0, slab(g, p), 0)),
+                pl.BlockSpec((2, both_chans, frame_len), lambda g, p: (0, p[0] ^ g, 0)),
+                pl.BlockSpec((2, both_chans, inputs), lambda g, p: (0, p[0] ^ g, 0)),
             ],
-            out_specs=[
-                pl.BlockSpec((1, chans, ROWS, inputs), lambda g, p: (jnp.minimum(g, slabs - 1), 0, 0, 0)),
-                pl.BlockSpec((1, chans, ROWS, inputs), lambda g, p: (jnp.maximum(g - slabs, 0), 0, 0, 0)),
-            ],
+            out_specs=[whole] * (2 * slabs),
             scratch_shapes=[
-                pltpu.VMEM((CHUNK * inputs, frame_len), jnp.bfloat16),
-                pltpu.VMEM((ROWS * chans, inputs), jnp.float32),
+                pltpu.VMEM((frame_len, CHUNK * inputs), jnp.bfloat16),
+                pltpu.VMEM((ROWS * PITCH, inputs), jnp.float32),
             ],
         ),
-        out_shape=[out, out],
-        compiler_params=pltpu.CompilerParams(vmem_limit_bytes=40 << 20),
+        out_shape=[out] * (2 * slabs),
+        compiler_params=pltpu.CompilerParams(vmem_limit_bytes=48 << 20),
         cost_estimate=pl.CostEstimate(flops=flops, bytes_accessed=24 << 20, transcendentals=0),
     )(place, samples, window, table, gains)
+    return outs[:slabs], outs[slabs:]
 
 
 def pair_kernel(scale, parts, where_ref, *refs):
@@ -243,12 +249,17 @@
         tiles = []
         for near, mine, far in sides:
             tiles.append(
-                [jnp.where(near, m[0, chan], f[0, chan]).astype(jnp.float32) for m, f in zip(mine, far)]
+                [jnp.where(near, m[0, chan], f[0, chan]) for m, f in zip(mine, far)]
             )
-        first = jnp.concatenate(tiles[0], 0).astype(jnp.bfloat16)
-        second = jnp.concatenate(tiles[1], 0).astype(jnp.bfloat16)
+        first = jnp.concatenate(tiles[0], 0)
+        second = jnp.concatenate(tiles[1], 0)
         swapped = jnp.concatenate(
-            [piece for x in tiles[1] for piece in (-x[CHUNK:], x[:CHUNK])], 0
+            [
+                piece
+                for x in (tile.astype(jnp.float32) for tile in tiles[1])
+                for piece in (-x[CHUNK:], x[:CHUNK])
+            ],
+            0,
         ).astype(jnp.bfloat16)
         both = lax.dot_general(
             first,
@@ -260,7 +271,7 @@
         out_ref[1, chan, 0] = both[:, BLOCK:]
         return carry
 
-    lax.fori_loop(0, out_ref.shape[1], one, 0, unroll=4)
+    lax.fori_loop(0, out_ref.shape[1], one, 0, unroll=16)
 
 
 def pair_products(where, mine, far, slots, scale):
@@ -293,11 +304,15 @@
     table = jnp.asarray(table_rows(samples.shape[2], NCH))
     early = part == 0
 
-    def made(first):
-        return voltage_chunk(place, samples, window, table, channel_gains, first)
-
-    def across(block):
-        return lax.ppermute(block, "tm", [(0, 1), (1, 0)])
+    def made(first, after=()):
+        block, *_ = lax.optimization_barrier((samples, *after))
+        return voltage_chunk(place, block, window, table, channel_gains, first)
+
+    def across(pieces, route):
+        moved = [None] * 4
+        for d in (3, 2, 1, 0):
+            moved[d] = lax.ppermute(pieces[d], "tm", route)
+        return moved
 
     def spread(pieces):
         moved = [pieces[0]]
@@ -310,18 +325,18 @@
         return (a.astype(jnp.float32) + b.astype(jnp.float32)).astype(jnp.bfloat16)
 
     mine, far = [], []
+    ready = ()
     for chunk in range(spectra // CHUNK):
-        other, own = made(chunk * CHUNK)
-        got = across(other)
-        other_tail, own_tail = made(spectra + chunk * CHUNK)
-        got_tail = lax.ppermute(other_tail, "tm", [(0, 1)])
-        for pieces in (
-            [jnp.where(early, own[d], got[d]) for d in range(4)],
-            [
-                jnp.where(early, added(got[d], own_tail[d]), added(own[d], got_tail[d]))
-                for d in range(4)
-            ],
-        ):
+        other, own = made(chunk * CHUNK, ready)
+        got = across(other, [(0, 1), (1, 0)])
+        now = [jnp.where(early, own[d], got[d]) for d in range(4)]
+        other_tail, own_tail = made(spectra + chunk * CHUNK, ready + (now[3],) if chunk == 0 else ready)
+        got_tail = across(other_tail, [(0, 1)])
+        ready = (now[2], now[1])
+        later = [
+            jnp.where(early, added(got[d], own_tail[d]), added(own[d], got_tail[d])) for d in range(4)
+        ]
+        for pieces in (now, later):
             a, b = spread(pieces)
             mine.append(a)
             far.append(b)

time: 386 us -> 337 us (0.87)
  waiting for transfers between devices: 186 us -> 117 us
  starting transfers between devices: 30.1 us -> 91 us
  Pallas kernels: 141 us -> 109 us
  local copies, waits for them, and re-layouts: 6.64 us -> 2.63 us
    ppermute x12, waiting for transfers between devices: 112 us -> 19.6 us  [spread(): lax.ppermute(pieces[d], 'chan', [(i, i ^ d) for i in range(4)])]
    ppermute x4, starting transfers between devices: 5.49 us -> 59.4 us  [spread(): return (mine, lax.ppermute(mine, 'blk', [(0, 1), (1, 0)]))]
    pallas_call x4, Pallas kernels: 115 us -> 86.8 us  [voltage_chunk(): pl.pallas_call(functools.partial(voltage_kernel, first), grid_spec=pltpu....]
    ppermute x4 -> x16, waiting for transfers between devices: 70.9 us -> 93.2 us  [across(): moved[d] = lax.ppermute(pieces[d], 'tm', route)]
    ppermute x4 -> x16, starting transfers between devices: 9.43 us -> 19.7 us  [across(): moved[d] = lax.ppermute(pieces[d], 'tm', route)]
    pallas_call x1, Pallas kernels: 26.1 us -> 22 us  [pair_products(): pl.pallas_call(functools.partial(pair_kernel, scale, parts), grid_spec=pl...]
    unnamed x18 -> x6, local copies, waits for them, and re-layouts: 6.45 us -> 2.45 us
    another operation x4 -> x6, other arithmetic: 5.12 us -> 8.9 us  [spread(): mine = jnp.stack(moved, 0)]
  transfers between devices with their start and end apart: 20 -> 32, of which waited for: 9 -> 17; matrix products, arithmetic and copies ran while one was open for 4% -> 5% of each run, Pallas kernels for 23% -> 20%
where the time goes in v2:
time: 337 us; the launch traced here: 335 us
  waiting for transfers between devices  117 us (35%)
  Pallas kernels  109 us (32%)
  starting transfers between devices  91 us (27%)
  other arithmetic  15.2 us (5%)
    ppermute x16, waiting for transfers between devices, across(): moved[d] = lax.ppermute(pieces[d], 'tm', route)  93.2 us
    pallas_call x4, Pallas kernels, voltage_chunk(): pl.pallas_call(functools.partial(voltage_kernel, first), grid_spec=pltpu....  86.8 us
    ppermute x4, starting transfers between devices, spread(): return (mine, lax.ppermute(mine, 'blk', [(0, 1), (1, 0)]))  59.4 us
    pallas_call x1, Pallas kernels, pair_products(): pl.pallas_call(functools.partial(pair_kernel, scale, parts), grid_spec=pl...  22 us
    ppermute x16, starting transfers between devices, across(): moved[d] = lax.ppermute(pieces[d], 'tm', route)  19.7 us
    ppermute x12, waiting for transfers between devices, spread(): lax.ppermute(pieces[d], 'chan', [(i, i ^ d) for i in range(4)])  19.6 us
    ppermute x12, starting transfers between devices, spread(): lax.ppermute(pieces[d], 'chan', [(i, i ^ d) for i in range(4)])  11.9 us
    another operation x6, other arithmetic, spread(): mine = jnp.stack(moved, 0)  8.9 us
  transfers between devices with their start and end apart: 32, of which 17 were waited for; matrix products, arithmetic and copies ran while one was open for 5% of the time, Pallas kernels for 20%

profile of v2, /device:TPU:19, one launch (start us, length us, event | category | flops | bytes accessed | tf_op | source)
XLA Modules:
  0.0 334.9 jit_solution(2056036355043019900)
XLA Ops:
  0.1 1.2 copy-done
  1.3 20.0 %shard_map.55 = (bf16[128,16,128]{2,1,0:T(8,128)(2,1)S(1)}, bf16[128,16,128]{2,1,0:T(8,128)(2,1)}, bf16[128,16,128]{2,1,0:T(8,128)(2,1)S(1)}, bf16[128,16,128]{2...) custom-call(s32[2]{0:T(128)S(1)} %pad_add_fusion.1.place_ref, ...), custom_call_target="tpu_custom_call" | custom-call | flops 8589934592 | bytes 25165824 | tf_op jit(solution)/shard_map/pallas_call | solution.py:214
  21.3 0.3 collective-permute-start.5
  21.5 1.2 collective-permute-start.1
  22.7 11.6 %collective-permute-done.5 = bf16[128,16,128]{2,1,0:T(8,128)(2,1)} collective-permute-done((bf16[128,16,128]{2,1,0:T(8,128)(2,1)}, bf16[128,16,128]{2,1,0:T(8,128)(2,1)}, u32[]{:S(2)}, u32[]{:S(2)}) %collective-permute-start.5) | collective-permute-done | bytes 524320 | tf_op jit(solution)/shard_map/ppermute | solution.py:314
  34.4 1.1 broadcast_select_fusion.3
  35.5 1.2 copy-done.1
  36.7 23.7 %shard_map.56 = (bf16[128,16,128]{2,1,0:T(8,128)(2,1)S(1)}, bf16[128,16,128]{2,1,0:T(8,128)(2,1)S(1)}, bf16[128,16,128]{2,1,0:T(8,128)(2,1)S(1)}, bf16[128,16,12...) custom-call(s32[2]{0:T(128)S(1)} %pad_add_fusion.1.place_ref, ...), custom_call_target="tpu_custom_call" | custom-call | flops 8589934592 | bytes 25165824 | tf_op jit(solution)/shard_map/pallas_call | solution.py:214
  60.4 1.3 collective-permute-start.8
  61.7 2.2 collective-permute-start.3
  63.9 1.3 collective-permute-start.10
  65.2 2.2 collective-permute-start
  67.4 0.2 collective-permute-start.6
  67.6 5.5 %collective-permute-done.8 = bf16[128,16,128]{2,1,0:T(8,128)(2,1)S(1)} collective-permute-done((bf16[128,16,128]{2,1,0:T(8,128)(2,1)S(1)}, bf16[128,16,128]{2,1,0:T(8,128)(2,1)S(1)}, u32[]{:S(2)}, u32[]{:S(2)}) %collective-permute-start.8) | collective-permute-done | bytes 524320 | tf_op jit(solution)/shard_map/ppermute | solution.py:314
  73.1 1.3 collective-permute-start.7
  74.3 2.4 fusion.2
  76.8 7.6 %collective-permute-done.3 = bf16[128,16,128]{2,1,0:T(8,128)(2,1)S(1)} collective-permute-done((bf16[128,16,128]{2,1,0:T(8,128)(2,1)S(1)}, bf16[128,16,128]{2,1,0:T(8,128)(2,1)S(1)}, u32[]{:S(2)}, u32[]{:S(2)}) %collective-permute-start.3) | collective-permute-done | bytes 524320 | tf_op jit(solution)/shard_map/ppermute | solution.py:314
  84.4 1.3 collective-permute-start.12
  85.7 9.8 %collective-permute-done.10 = bf16[128,16,128]{2,1,0:T(8,128)(2,1)S(1)} collective-permute-done((bf16[128,16,128]{2,1,0:T(8,128)(2,1)S(1)}, bf16[128,16,128]{2,1,0:T(8,128)(2,1)S(1)}, u32[]{:S(2)}, u32[]{:S(2)}) %collective-permute-start.10) | collective-permute-done | bytes 524320 | tf_op jit(solution)/shard_map/ppermute | solution.py:314
  95.5 1.3 collective-permute-start.9
  96.8 0.3 fusion.3
  97.2 18.8 %shard_map.58 = (bf16[128,16,128]{2,1,0:T(8,128)(2,1)S(1)}, bf16[128,16,128]{2,1,0:T(8,128)(2,1)S(1)}, bf16[128,16,128]{2,1,0:T(8,128)(2,1)S(1)}, bf16[128,16,12...) custom-call(s32[2]{0:T(128)S(1)} %pad_add_fusion.1.place_ref, ...), custom_call_target="tpu_custom_call" | custom-call | flops 8589934592 | bytes 25165824 | tf_op jit(solution)/shard_map/pallas_call | solution.py:214
  116.0 24.3 %shard_map.57 = (bf16[128,16,128]{2,1,0:T(8,128)(2,1)S(1)}, bf16[128,16,128]{2,1,0:T(8,128)(2,1)S(1)}, bf16[128,16,128]{2,1,0:T(8,128)(2,1)S(1)}, bf16[128,16,12...) custom-call(s32[2]{0:T(128)S(1)} %pad_add_fusion.1.place_ref, ...), custom_call_target="tpu_custom_call" | custom-call | flops 8589934592 | bytes 25165824 | tf_op jit(solution)/shard_map/pallas_call | solution.py:214
  140.3 0.3 collective-permute-start.2
  140.6 1.3 collective-permute-start.22
  141.9 2.2 collective-permute-start.15
  144.1 1.4 fusion.1
  145.4 0.1 collective-permute-start.11
  145.6 1.3 collective-permute-start.24
  146.9 1.6 collective-permute-done.2
  148.4 1.5 collective-permute-start.26
  149.9 0.9 collective-permute-done.22
  150.8 1.3 collective-permute-start.17
  152.1 7.6 %collective-permute-done.15 = bf16[128,16,128]{2,1,0:T(8,128)(2,1)S(1)} collective-permute-done((bf16[128,16,128]{2,1,0:T(8,128)(2,1)S(1)}, bf16[128,16,128]{2,1,0:T(8,128)(2,1)S(1)}, u32[]{:S(2)}, u32[]{:S(2)}) %collective-permute-start.15) | collective-permute-done | bytes 524320 | tf_op jit(solution)/shard_map/ppermute | solution.py:314
  159.7 1.3 fusion.4
  161.0 0.3 fusion.7
  161.4 0.5 collective-permute-start.4
  161.9 9.0 %collective-permute-done.24 = bf16[128,16,128]{2,1,0:T(8,128)(2,1)S(1)} collective-permute-done((bf16[128,16,128]{2,1,0:T(8,128)(2,1)S(1)}, bf16[128,16,128]{2,1,0:T(8,128)(2,1)S(1)}, u32[]{:S(2)}, u32[]{:S(2)}) %collective-permute-start.24) | collective-permute-done | bytes 524320 | tf_op jit(solution)/shard_map/ppermute | solution.py:314
  171.0 4.5 %collective-permute-start.13 = (bf16[128,16,128]{2,1,0:T(8,128)(2,1)S(1)}, bf16[128,16,128]{2,1,0:T(8,128)(2,1)S(1)}, u32[]{:S(2)}, u32[]{:S(2)}) collective-permute-start(bf16[128,16,128]{2,1,0:T(8,128)(2,1)S(1)} %fusion.4), channel_id=1, source_target_pairs={{0,12},{4,8},{8,4},{12,0},{1,13},{5,9},{9,5},{13,1},{2,14},{6,10},... | collective-permute-start | bytes 1572872 | tf_op jit(solution)/shard_map/ppermute | solution.py:320
  175.4 6.8 %collective-permute-done.26 = bf16[128,16,128]{2,1,0:T(8,128)(2,1)S(1)} collective-permute-done((bf16[128,16,128]{2,1,0:T(8,128)(2,1)S(1)}, bf16[128,16,128]{2,1,0:T(8,128)(2,1)S(1)}, u32[]{:S(2)}, u32[]{:S(2)}) %collective-permute-start.26) | collective-permute-done | bytes 524320 | tf_op jit(solution)/shard_map/ppermute | solution.py:314
  182.2 1.3 collective-permute-start.21
  183.5 9.9 %collective-permute-done.17 = bf16[128,16,128]{2,1,0:T(8,128)(2,1)S(1)} collective-permute-done((bf16[128,16,128]{2,1,0:T(8,128)(2,1)S(1)}, bf16[128,16,128]{2,1,0:T(8,128)(2,1)S(1)}, u32[]{:S(2)}, u32[]{:S(2)}) %collective-permute-start.17) | collective-permute-done | bytes 524320 | tf_op jit(solution)/shard_map/ppermute | solution.py:314
  193.4 11.2 %collective-permute-done.19 = bf16[128,16,128]{2,1,0:T(8,128)(2,1)S(1)} collective-permute-done((bf16[128,16,128]{2,1,0:T(8,128)(2,1)S(1)}, bf16[128,16,128]{2,1,0:T(8,128)(2,1)S(1)}, u32[]{:S(2)}, u32[]{:S(2)}) %collective-permute-start.19) | collective-permute-done | bytes 524320 | tf_op jit(solution)/shard_map/ppermute | solution.py:314
  204.7 1.3 collective-permute-start.16
  205.9 0.3 fusion.8
  206.3 0.3 fusion.9
  206.6 0.2 collective-permute-start.18
  206.8 4.7 %collective-permute-done.13 = bf16[128,16,128]{2,1,0:T(8,128)(2,1)S(1)} collective-permute-done((bf16[128,16,128]{2,1,0:T(8,128)(2,1)S(1)}, bf16[128,16,128]{2,1,0:T(8,128)(2,1)S(1)}, u32[]{:S(2)}, u32[]{:S(2)}) %collective-permute-start.13) | collective-permute-done | bytes 524320 | tf_op jit(solution)/shard_map/ppermute | solution.py:320
  211.5 1.3 pad_maximum_fusion.refs_0_.refs_8_
  212.8 3.1 collective-permute-done.21
  215.9 1.3 collective-permute-start.23
  217.2 10.0 %collective-permute-done.14 = bf16[128,16,128]{2,1,0:T(8,128)(2,1)S(1)} collective-permute-done((bf16[128,16,128]{2,1,0:T(8,128)(2,1)S(1)}, bf16[128,16,128]{2,1,0:T(8,128)(2,1)S(1)}, u32[]{:S(2)}, u32[]{:S(2)}) %collective-permute-start.14) | collective-permute-done | bytes 524320 | tf_op jit(solution)/shard_map/ppermute | solution.py:314
  227.2 2.4 collective-permute-start.27
  229.6 2.6 pad_maximum_fusion.1.refs_1_.refs_9_
  232.2 0.3 fusion.6
  232.6 43.5 %collective-permute-start.29 = (bf16[4,128,16,128]{3,2,1,0:T(8,128)(2,1)}, bf16[4,128,16,128]{3,2,1,0:T(8,128)(2,1)}, u32[]{:S(2)}, u32[]{:S(2)}) collective-permute-start(bf16[4,128,16,128]{3,2,1,0:T(8,128)(2,1)} %pad_maximum_fusion.1.refs_1_.refs_9_), channel_id=1, source_target_pairs={{0,1},{1,0},{2,3},{3,2},{4,5},{5,4},{6,7},{7,6},{8,9},{9,8},{10,11... | collective-permute-start | bytes 6291464 | tf_op jit(solution)/shard_map/ppermute | solution.py:322
  276.1 2.9 collective-permute-done.20
  279.0 10.5 %collective-permute-start.28 = (bf16[4,128,16,128]{3,2,1,0:T(8,128)(2,1)S(1)}, bf16[4,128,16,128]{3,2,1,0:T(8,128)(2,1)}, u32[]{:S(2)}, u32[]{:S(2)}) collective-permute-start(bf16[4,128,16,128]{3,2,1,0:T(8,128)(2,1)S(1)} %pad_maximum_fusion.refs_0_.refs_8_), channel_id=1, source_target_pairs={{0,1},{1,0},{2,3},{3,2},{4,5},{5,4},{6,7},{7,6},{8,9},{9,8},{10,11... | collective-permute-start | bytes 6291464 | tf_op jit(solution)/shard_map/ppermute | solution.py:322
  289.4 1.6 pad_maximum_fusion.2.refs_2_.refs_10_
  291.0 10.4 %collective-permute-done.27 = bf16[128,16,128]{2,1,0:T(8,128)(2,1)S(1)} collective-permute-done((bf16[128,16,128]{2,1,0:T(8,128)(2,1)S(1)}, bf16[128,16,128]{2,1,0:T(8,128)(2,1)S(1)}, u32[]{:S(2)}, u32[]{:S(2)}) %collective-permute-start.27) | collective-permute-done | bytes 524320 | tf_op jit(solution)/shard_map/ppermute | solution.py:320
  301.5 1.6 pad_maximum_fusion.3.refs_3_.refs_11_
  303.1 5.4 %collective-permute-start.31 = (bf16[4,128,16,128]{3,2,1,0:T(8,128)(2,1)}, bf16[4,128,16,128]{3,2,1,0:T(8,128)(2,1)}, u32[]{:S(2)}, u32[]{:S(2)}) collective-permute-start(bf16[4,128,16,128]{3,2,1,0:T(8,128)(2,1)} %pad_maximum_fusion.3.refs_3_.refs_11_), channel_id=1, source_target_pairs={{0,1},{1,0},{2,3},{3,2},{4,5},{5,4},{6,7},{7,6},{8,9},{9,8},{10,11... | collective-permute-start | bytes 6291464 | tf_op jit(solution)/shard_map/ppermute | solution.py:322
  308.8 3.9 %collective-permute-done.31.refs_7_.refs_15_ = bf16[4,128,16,128]{3,2,1,0:T(8,128)(2,1)} collective-permute-done((bf16[4,128,16,128]{3,2,1,0:T(8,128)(2,1)}, bf16[4,128,16,128]{3,2,1,0:T(8,128)(2,1)}, u32[]{:S(2)}, u32[]{:S(2)}) %collective-permute-start.31) | collective-permute-done | bytes 2097184 | tf_op jit(solution)/shard_map/ppermute | solution.py:322
  312.7 22.0 %shard_map.59 = f32[2,128,2,128,128]{4,3,2,1,0:T(8,128)} custom-call(s32[8]{0:T(128)S(1)} %reshape.3.where_ref, bf16[4,128,16,128]{3,2,1,0:T(8,128)(2,1)S(1)} %pad_maximum_fusion.refs_0_.refs_8_, bf16[4,128,16,128]{3,2,1,0:T(8,128)(2,1)} %pad_maximum_fusion.1.refs_1_.refs_9_, bf16[4,128,16,128]{3,2,1,0:T(8,128)(2,1)} %pad_maximum_fusion.2.refs_2_.refs_10_, ...), custom_call_target="tpu_custom_call" | custom-call | flops 4294967296 | bytes 52428800 | tf_op jit(solution)/shard_map/pallas_call | solution.py:285
  (29 shorter events, 0.4 us)
Async XLA Ops:
  0.1 1.2 copy-start
  21.3 13.1 %collective-permute-start.5 = (bf16[128,16,128]{2,1,0:T(8,128)(2,1)}, bf16[128,16,128]{2,1,0:T(8,128)(2,1)}, u32[]{:S(2)}, u32[]{:S(2)}) collective-permute-start(bf16[128,16,128]{2,1,0:T(8,128)(2,1)} %get-tuple-element.46), channel_id=1, source_target_pairs={{0,2},{2,0},{1,3},{3,1},{4,6},{6,4},{5,7},{7,5},{8,10},{10,8},{9,1... | collective-permute-start | bytes 1572872 | tf_op jit(solution)/shard_map/ppermute | solution.py:314
  21.5 45.8 %collective-permute-start.1 = (bf16[128,16,128]{2,1,0:T(8,128)(2,1)}, bf16[128,16,128]{2,1,0:T(8,128)(2,1)}, u32[]{:S(2)}, u32[]{:S(2)}) collective-permute-start(bf16[128,16,128]{2,1,0:T(8,128)(2,1)} %get-tuple-element.42), channel_id=1, source_target_pairs={{0,2},{2,0},{1,3},{3,1},{4,6},{6,4},{5,7},{7,5},{8,10},{10,8},{9,1... | collective-permute-start | bytes 1572872 | tf_op jit(solution)/shard_map/ppermute | solution.py:314
  35.5 1.2 copy-start.1
  60.4 12.6 %collective-permute-start.8 = (bf16[128,16,128]{2,1,0:T(8,128)(2,1)S(1)}, bf16[128,16,128]{2,1,0:T(8,128)(2,1)S(1)}, u32[]{:S(2)}, u32[]{:S(2)}) collective-permute-start(bf16[128,16,128]{2,1,0:T(8,128)(2,1)S(1)} %get-tuple-element.51), channel_id=1, source_target_pairs={{0,2},{1,3},{4,6},{5,7},{8,10},{9,11},{12,14},{13,15},{16,18},{17,... | collective-permute-start | bytes 1572872 | tf_op jit(solution)/shard_map/ppermute | solution.py:314
  61.7 22.7 %collective-permute-start.3 = (bf16[128,16,128]{2,1,0:T(8,128)(2,1)S(1)}, bf16[128,16,128]{2,1,0:T(8,128)(2,1)S(1)}, u32[]{:S(2)}, u32[]{:S(2)}) collective-permute-start(bf16[128,16,128]{2,1,0:T(8,128)(2,1)S(1)} %get-tuple-element.44), channel_id=1, source_target_pairs={{0,2},{2,0},{1,3},{3,1},{4,6},{6,4},{5,7},{7,5},{8,10},{10,8},{9,1... | collective-permute-start | bytes 1572872 | tf_op jit(solution)/shard_map/ppermute | solution.py:314
  63.9 31.6 %collective-permute-start.10 = (bf16[128,16,128]{2,1,0:T(8,128)(2,1)S(1)}, bf16[128,16,128]{2,1,0:T(8,128)(2,1)S(1)}, u32[]{:S(2)}, u32[]{:S(2)}) collective-permute-start(bf16[128,16,128]{2,1,0:T(8,128)(2,1)S(1)} %get-tuple-element.53), channel_id=1, source_target_pairs={{0,2},{1,3},{4,6},{5,7},{8,10},{9,11},{12,14},{13,15},{16,18},{17,... | collective-permute-start | bytes 1572872 | tf_op jit(solution)/shard_map/ppermute | solution.py:314
  65.2 75.1 %collective-permute-start = (bf16[128,16,128]{2,1,0:T(8,128)(2,1)S(1)}, bf16[128,16,128]{2,1,0:T(8,128)(2,1)S(1)}, u32[]{:S(2)}, u32[]{:S(2)}) collective-permute-start(bf16[128,16,128]{2,1,0:T(8,128)(2,1)S(1)} %get-tuple-element.40), channel_id=1, source_target_pairs={{0,2},{2,0},{1,3},{3,1},{4,6},{6,4},{5,7},{7,5},{8,10},{10,8},{9,1... | collective-permute-start | bytes 1572872 | tf_op jit(solution)/shard_map/ppermute | solution.py:314
  67.4 73.2 %collective-permute-start.6 = (bf16[128,16,128]{2,1,0:T(8,128)(2,1)S(1)}, bf16[128,16,128]{2,1,0:T(8,128)(2,1)}, u32[]{:S(2)}, u32[]{:S(2)}) collective-permute-start(bf16[128,16,128]{2,1,0:T(8,128)(2,1)S(1)} %broadcast_select_fusion.3), channel_id=1, source_target_pairs={{0,12},{4,8},{8,4},{12,0},{1,13},{5,9},{9,5},{13,1},{2,14},{6,10},... | collective-permute-start | bytes 1572872 | tf_op jit(solution)/shard_map/ppermute | solution.py:320
  73.1 68.8 %collective-permute-start.7 = (bf16[128,16,128]{2,1,0:T(8,128)(2,1)S(1)}, bf16[128,16,128]{2,1,0:T(8,128)(2,1)}, u32[]{:S(2)}, u32[]{:S(2)}) collective-permute-start(bf16[128,16,128]{2,1,0:T(8,128)(2,1)S(1)} %get-tuple-element.49), channel_id=1, source_target_pairs={{0,2},{1,3},{4,6},{5,7},{8,10},{9,11},{12,14},{13,15},{16,18},{17,... | collective-permute-start | bytes 1572872 | tf_op jit(solution)/shard_map/ppermute | solution.py:314
  84.4 61.0 %collective-permute-start.12 = (bf16[128,16,128]{2,1,0:T(8,128)(2,1)S(1)}, bf16[128,16,128]{2,1,0:T(8,128)(2,1)S(1)}, u32[]{:S(2)}, u32[]{:S(2)}) collective-permute-start(bf16[128,16,128]{2,1,0:T(8,128)(2,1)S(1)} %get-tuple-element.55), channel_id=1, source_target_pairs={{0,2},{1,3},{4,6},{5,7},{8,10},{9,11},{12,14},{13,15},{16,18},{17,... | collective-permute-start | bytes 1572872 | tf_op jit(solution)/shard_map/ppermute | solution.py:314
  95.5 50.0 %collective-permute-start.9 = (bf16[128,16,128]{2,1,0:T(8,128)(2,1)}, bf16[128,16,128]{2,1,0:T(8,128)(2,1)}, u32[]{:S(2)}, u32[]{:S(2)}) collective-permute-start(bf16[128,16,128]{2,1,0:T(8,128)(2,1)} %get-tuple-element.83), channel_id=1, source_target_pairs={{0,4},{4,0},{8,12},{12,8},{1,5},{5,1},{9,13},{13,9},{2,6},{6,2},{1... | collective-permute-start | bytes 1572872 | tf_op jit(solution)/shard_map/ppermute | solution.py:320
  140.3 8.1 %collective-permute-start.2 = (bf16[128,16,128]{2,1,0:T(8,128)(2,1)S(1)}, bf16[128,16,128]{2,1,0:T(8,128)(2,1)S(1)}, u32[]{:S(2)}, u32[]{:S(2)}) collective-permute-start(bf16[128,16,128]{2,1,0:T(8,128)(2,1)S(1)} %get-tuple-element.84), channel_id=1, source_target_pairs={{0,4},{4,0},{8,12},{12,8},{1,5},{5,1},{9,13},{13,9},{2,6},{6,2},{1... | collective-permute-start | bytes 1572872 | tf_op jit(solution)/shard_map/ppermute | solution.py:320
  140.6 10.2 %collective-permute-start.22 = (bf16[128,16,128]{2,1,0:T(8,128)(2,1)S(1)}, bf16[128,16,128]{2,1,0:T(8,128)(2,1)S(1)}, u32[]{:S(2)}, u32[]{:S(2)}) collective-permute-start(bf16[128,16,128]{2,1,0:T(8,128)(2,1)S(1)} %get-tuple-element.68), channel_id=1, source_target_pairs={{0,2},{1,3},{4,6},{5,7},{8,10},{9,11},{12,14},{13,15},{16,18},{17,... | collective-permute-start | bytes 1572872 | tf_op jit(solution)/shard_map/ppermute | solution.py:314
  141.9 17.8 %collective-permute-start.15 = (bf16[128,16,128]{2,1,0:T(8,128)(2,1)S(1)}, bf16[128,16,128]{2,1,0:T(8,128)(2,1)S(1)}, u32[]{:S(2)}, u32[]{:S(2)}) collective-permute-start(bf16[128,16,128]{2,1,0:T(8,128)(2,1)S(1)} %get-tuple-element.60), channel_id=1, source_target_pairs={{0,2},{2,0},{1,3},{3,1},{4,6},{6,4},{5,7},{7,5},{8,10},{10,8},{9,1... | collective-permute-start | bytes 1572872 | tf_op jit(solution)/shard_map/ppermute | solution.py:314
  145.4 15.9 %collective-permute-start.11 = (bf16[128,16,128]{2,1,0:T(8,128)(2,1)S(1)}, bf16[128,16,128]{2,1,0:T(8,128)(2,1)S(1)}, u32[]{:S(2)}, u32[]{:S(2)}) collective-permute-start(bf16[128,16,128]{2,1,0:T(8,128)(2,1)S(1)} %get-tuple-element.85), channel_id=1, source_target_pairs={{0,8},{4,12},{8,0},{12,4},{1,9},{5,13},{9,1},{13,5},{2,10},{6,14},... | collective-permute-start | bytes 1572872 | tf_op jit(solution)/shard_map/ppermute | solution.py:320
  145.6 25.4 %collective-permute-start.24 = (bf16[128,16,128]{2,1,0:T(8,128)(2,1)S(1)}, bf16[128,16,128]{2,1,0:T(8,128)(2,1)S(1)}, u32[]{:S(2)}, u32[]{:S(2)}) collective-permute-start(bf16[128,16,128]{2,1,0:T(8,128)(2,1)S(1)} %get-tuple-element.70), channel_id=1, source_target_pairs={{0,2},{1,3},{4,6},{5,7},{8,10},{9,11},{12,14},{13,15},{16,18},{17,... | collective-permute-start | bytes 1572872 | tf_op jit(solution)/shard_map/ppermute | solution.py:314
  148.4 33.8 %collective-permute-start.26 = (bf16[128,16,128]{2,1,0:T(8,128)(2,1)S(1)}, bf16[128,16,128]{2,1,0:T(8,128)(2,1)S(1)}, u32[]{:S(2)}, u32[]{:S(2)}) collective-permute-start(bf16[128,16,128]{2,1,0:T(8,128)(2,1)S(1)} %get-tuple-element.72), channel_id=1, source_target_pairs={{0,2},{1,3},{4,6},{5,7},{8,10},{9,11},{12,14},{13,15},{16,18},{17,... | collective-permute-start | bytes 1572872 | tf_op jit(solution)/shard_map/ppermute | solution.py:314
  150.8 42.6 %collective-permute-start.17 = (bf16[128,16,128]{2,1,0:T(8,128)(2,1)S(1)}, bf16[128,16,128]{2,1,0:T(8,128)(2,1)S(1)}, u32[]{:S(2)}, u32[]{:S(2)}) collective-permute-start(bf16[128,16,128]{2,1,0:T(8,128)(2,1)S(1)} %get-tuple-element.62), channel_id=1, source_target_pairs={{0,2},{2,0},{1,3},{3,1},{4,6},{6,4},{5,7},{7,5},{8,10},{10,8},{9,1... | collective-permute-start | bytes 1572872 | tf_op jit(solution)/shard_map/ppermute | solution.py:314
  159.7 44.9 %collective-permute-start.19 = (bf16[128,16,128]{2,1,0:T(8,128)(2,1)S(1)}, bf16[128,16,128]{2,1,0:T(8,128)(2,1)S(1)}, u32[]{:S(2)}, u32[]{:S(2)}) collective-permute-start(bf16[128,16,128]{2,1,0:T(8,128)(2,1)S(1)} %get-tuple-element.64), channel_id=1, source_target_pairs={{0,2},{2,0},{1,3},{3,1},{4,6},{6,4},{5,7},{7,5},{8,10},{10,8},{9,1... | collective-permute-start | bytes 1572872 | tf_op jit(solution)/shard_map/ppermute | solution.py:314
  161.4 45.2 %collective-permute-start.4 = (bf16[128,16,128]{2,1,0:T(8,128)(2,1)S(1)}, bf16[128,16,128]{2,1,0:T(8,128)(2,1)S(1)}, u32[]{:S(2)}, u32[]{:S(2)}) collective-permute-start(bf16[128,16,128]{2,1,0:T(8,128)(2,1)S(1)} %get-tuple-element.86), channel_id=1, source_target_pairs={{0,8},{4,12},{8,0},{12,4},{1,9},{5,13},{9,1},{13,5},{2,10},{6,14},... | collective-permute-start | bytes 1572872 | tf_op jit(solution)/shard_map/ppermute | solution.py:320
  171.0 40.6 %collective-permute-start.13 = (bf16[128,16,128]{2,1,0:T(8,128)(2,1)S(1)}, bf16[128,16,128]{2,1,0:T(8,128)(2,1)S(1)}, u32[]{:S(2)}, u32[]{:S(2)}) collective-permute-start(bf16[128,16,128]{2,1,0:T(8,128)(2,1)S(1)} %fusion.4), channel_id=1, source_target_pairs={{0,12},{4,8},{8,4},{12,0},{1,13},{5,9},{9,5},{13,1},{2,14},{6,10},... | collective-permute-start | bytes 1572872 | tf_op jit(solution)/shard_map/ppermute | solution.py:320
  182.2 33.7 %collective-permute-start.21 = (bf16[128,16,128]{2,1,0:T(8,128)(2,1)S(1)}, bf16[128,16,128]{2,1,0:T(8,128)(2,1)S(1)}, u32[]{:S(2)}, u32[]{:S(2)}) collective-permute-start(bf16[128,16,128]{2,1,0:T(8,128)(2,1)S(1)} %get-tuple-element.66), channel_id=1, source_target_pairs={{0,2},{1,3},{4,6},{5,7},{8,10},{9,11},{12,14},{13,15},{16,18},{17,... | collective-permute-start | bytes 1572872 | tf_op jit(solution)/shard_map/ppermute | solution.py:314
  193.4 33.7 %collective-permute-start.14 = (bf16[128,16,128]{2,1,0:T(8,128)(2,1)S(1)}, bf16[128,16,128]{2,1,0:T(8,128)(2,1)S(1)}, u32[]{:S(2)}, u32[]{:S(2)}) collective-permute-start(bf16[128,16,128]{2,1,0:T(8,128)(2,1)S(1)} %get-tuple-element.58), channel_id=1, source_target_pairs={{0,2},{2,0},{1,3},{3,1},{4,6},{6,4},{5,7},{7,5},{8,10},{10,8},{9,1... | collective-permute-start | bytes 1572872 | tf_op jit(solution)/shard_map/ppermute | solution.py:314
  204.7 22.5 %collective-permute-start.16 = (bf16[128,16,128]{2,1,0:T(8,128)(2,1)S(1)}, bf16[128,16,128]{2,1,0:T(8,128)(2,1)S(1)}, u32[]{:S(2)}, u32[]{:S(2)}) collective-permute-start(bf16[128,16,128]{2,1,0:T(8,128)(2,1)S(1)} %get-tuple-element.76), channel_id=1, source_target_pairs={{0,4},{4,0},{8,12},{12,8},{1,5},{5,1},{9,13},{13,9},{2,6},{6,2},{1... | collective-permute-start | bytes 1572872 | tf_op jit(solution)/shard_map/ppermute | solution.py:320
  206.6 25.9 %collective-permute-start.18 = (bf16[128,16,128]{2,1,0:T(8,128)(2,1)S(1)}, bf16[128,16,128]{2,1,0:T(8,128)(2,1)S(1)}, u32[]{:S(2)}, u32[]{:S(2)}) collective-permute-start(bf16[128,16,128]{2,1,0:T(8,128)(2,1)S(1)} %get-tuple-element.78), channel_id=1, source_target_pairs={{0,8},{4,12},{8,0},{12,4},{1,9},{5,13},{9,1},{13,5},{2,10},{6,14},... | collective-permute-start | bytes 1572872 | tf_op jit(solution)/shard_map/ppermute | solution.py:320
  211.5 67.5 %collective-permute-start.20 = (bf16[128,16,128]{2,1,0:T(8,128)(2,1)S(1)}, bf16[128,16,128]{2,1,0:T(8,128)(2,1)S(1)}, u32[]{:S(2)}, u32[]{:S(2)}) collective-permute-start(bf16[128,16,128]{2,1,0:T(8,128)(2,1)S(1)} %get-tuple-element.80), channel_id=1, source_target_pairs={{0,12},{4,8},{8,4},{12,0},{1,13},{5,9},{9,5},{13,1},{2,14},{6,10},... | collective-permute-start | bytes 1572872 | tf_op jit(solution)/shard_map/ppermute | solution.py:320
  215.9 75.1 %collective-permute-start.23 = (bf16[128,16,128]{2,1,0:T(8,128)(2,1)S(1)}, bf16[128,16,128]{2,1,0:T(8,128)(2,1)S(1)}, u32[]{:S(2)}, u32[]{:S(2)}) collective-permute-start(bf16[128,16,128]{2,1,0:T(8,128)(2,1)S(1)} %get-tuple-element.75), channel_id=1, source_target_pairs={{0,4},{4,0},{8,12},{12,8},{1,5},{5,1},{9,13},{13,9},{2,6},{6,2},{1... | collective-permute-start | bytes 1572872 | tf_op jit(solution)/shard_map/ppermute | solution.py:320
  227.1 63.9 %collective-permute-start.25 = (bf16[128,16,128]{2,1,0:T(8,128)(2,1)S(1)}, bf16[128,16,128]{2,1,0:T(8,128)(2,1)S(1)}, u32[]{:S(2)}, u32[]{:S(2)}) collective-permute-start(bf16[128,16,128]{2,1,0:T(8,128)(2,1)S(1)} %get-tuple-element.77), channel_id=1, source_target_pairs={{0,8},{4,12},{8,0},{12,4},{1,9},{5,13},{9,1},{13,5},{2,10},{6,14},... | collective-permute-start | bytes 1572872 | tf_op jit(solution)/shard_map/ppermute | solution.py:320
  227.2 74.3 %collective-permute-start.27 = (bf16[128,16,128]{2,1,0:T(8,128)(2,1)S(1)}, bf16[128,16,128]{2,1,0:T(8,128)(2,1)S(1)}, u32[]{:S(2)}, u32[]{:S(2)}) collective-permute-start(bf16[128,16,128]{2,1,0:T(8,128)(2,1)S(1)} %get-tuple-element.79), channel_id=1, source_target_pairs={{0,12},{4,8},{8,4},{12,0},{1,13},{5,9},{9,5},{13,1},{2,14},{6,10},... | collective-permute-start | bytes 1572872 | tf_op jit(solution)/shard_map/ppermute | solution.py:320
  232.6 76.2 %collective-permute-start.29 = (bf16[4,128,16,128]{3,2,1,0:T(8,128)(2,1)}, bf16[4,128,16,128]{3,2,1,0:T(8,128)(2,1)}, u32[]{:S(2)}, u32[]{:S(2)}) collective-permute-start(bf16[4,128,16,128]{3,2,1,0:T(8,128)(2,1)} %pad_maximum_fusion.1.refs_1_.refs_9_), channel_id=1, source_target_pairs={{0,1},{1,0},{2,3},{3,2},{4,5},{5,4},{6,7},{7,6},{8,9},{9,8},{10,11... | collective-permute-start | bytes 6291464 | tf_op jit(solution)/shard_map/ppermute | solution.py:322
  279.0 29.8 %collective-permute-start.28 = (bf16[4,128,16,128]{3,2,1,0:T(8,128)(2,1)S(1)}, bf16[4,128,16,128]{3,2,1,0:T(8,128)(2,1)}, u32[]{:S(2)}, u32[]{:S(2)}) collective-permute-start(bf16[4,128,16,128]{3,2,1,0:T(8,128)(2,1)S(1)} %pad_maximum_fusion.refs_0_.refs_8_), channel_id=1, source_target_pairs={{0,1},{1,0},{2,3},{3,2},{4,5},{5,4},{6,7},{7,6},{8,9},{9,8},{10,11... | collective-permute-start | bytes 6291464 | tf_op jit(solution)/shard_map/ppermute | solution.py:322
  291.0 17.7 %collective-permute-start.30 = (bf16[4,128,16,128]{3,2,1,0:T(8,128)(2,1)}, bf16[4,128,16,128]{3,2,1,0:T(8,128)(2,1)}, u32[]{:S(2)}, u32[]{:S(2)}) collective-permute-start(bf16[4,128,16,128]{3,2,1,0:T(8,128)(2,1)} %pad_maximum_fusion.2.refs_2_.refs_10_), channel_id=1, source_target_pairs={{0,1},{1,0},{2,3},{3,2},{4,5},{5,4},{6,7},{7,6},{8,9},{9,8},{10,11... | collective-permute-start | bytes 6291464 | tf_op jit(solution)/shard_map/ppermute | solution.py:322
  301.5 7.1 %copy-start.2 = (s32[2,2]{1,0:T(2,128)S(1)}, s32[2,2]{1,0:T(2,128)}, u32[]{:S(2)}) copy-start(s32[2,2]{1,0:T(2,128)} %param.7) | copy-start | bytes 52
  303.1 9.6 %collective-permute-start.31 = (bf16[4,128,16,128]{3,2,1,0:T(8,128)(2,1)}, bf16[4,128,16,128]{3,2,1,0:T(8,128)(2,1)}, u32[]{:S(2)}, u32[]{:S(2)}) collective-permute-start(bf16[4,128,16,128]{3,2,1,0:T(8,128)(2,1)} %pad_maximum_fusion.3.refs_3_.refs_11_), channel_id=1, source_target_pairs={{0,1},{1,0},{2,3},{3,2},{4,5},{5,4},{6,7},{7,6},{8,9},{9,8},{10,11... | collective-permute-start | bytes 6291464 | tf_op jit(solution)/shard_map/ppermute | solution.py:322

commit v3 on v2

--- a/solution.py
+++ b/solution.py
@@ -127,9 +127,10 @@
     return parts.astype(ml_dtypes.bfloat16)
 
 
-def voltage_kernel(first, place_ref, x_ref, w_ref, tab_ref, gain_ref, *refs):
+def voltage_kernel(first, cuts, place_ref, x_ref, w_ref, tab_ref, gain_ref, *refs):
     filt, turned = refs[-2:]
-    slabs = (len(refs) - 2) // 2
+    slabs = 4
+    others, owns = refs[:cuts], refs[cuts:-2]
     step = pl.program_id(0)
     spectra, inputs, frame_len = x_ref.shape
 
@@ -192,7 +193,8 @@
 
         @pl.when(step == slab)
         def _():
-            for out_ref, base in ((refs[slab], (1 - part) * chans), (refs[slabs + slab], part * chans)):
+            sent = others[slab * cuts // slabs].at[slab % (slabs // cuts)]
+            for out_ref, base in ((sent, (1 - part) * chans), (owns[slab], part * chans)):
 
                 def one(chan, carry):
                     out_ref[chan] = turned[pl.ds(base + chan, ROWS, stride=PITCH), :].astype(jnp.bfloat16)
@@ -204,35 +206,37 @@
 PITCH = 257
 
 
-def voltage_chunk(place, samples, window, table, gains, first):
+def voltage_chunk(place, samples, window, table, gains, first, cuts):
     spectra, inputs, frame_len = samples.shape
     slabs = 4
     both_chans = table.shape[1] // slabs
     out = jax.ShapeDtypeStruct((both_chans // 2, ROWS, inputs), jnp.bfloat16)
     flops = 2 * table.shape[1] * 2 * frame_len * CHUNK * inputs
     whole = pl.BlockSpec(out.shape, lambda g, p: (0, 0, 0))
+    twice = jax.ShapeDtypeStruct((slabs // cuts, *out.shape), jnp.bfloat16)
+    pair = pl.BlockSpec(twice.shape, lambda g, p: (0, 0, 0, 0))
     outs = pl.pallas_call(
-        functools.partial(voltage_kernel, first),
+        functools.partial(voltage_kernel, first, cuts),
         grid_spec=pltpu.PrefetchScalarGridSpec(
             num_scalar_prefetch=1,
             grid=(slabs,),
             in_specs=[
                 pl.BlockSpec((spectra, inputs, frame_len), lambda g, p: (0, 0, 0), pipeline_mode=pl.Buffered(1)),
                 pl.BlockSpec((TAPS, 8, frame_len), lambda g, p: (0, 0, 0), pipeline_mode=pl.Buffered(1)),
-                pl.BlockSpec((2, both_chans, frame_len), lambda g, p: (0, p[0] ^ g, 0)),
-                pl.BlockSpec((2, both_chans, inputs), lambda g, p: (0, p[0] ^ g, 0)),
+                pl.BlockSpec((2, both_chans, frame_len), lambda g, p: (0, p[0] ^ (slabs - 1 - g), 0)),
+                pl.BlockSpec((2, both_chans, inputs), lambda g, p: (0, p[0] ^ (slabs - 1 - g), 0)),
             ],
-            out_specs=[whole] * (2 * slabs),
+            out_specs=[pair] * cuts + [whole] * slabs,
             scratch_shapes=[
                 pltpu.VMEM((frame_len, CHUNK * inputs), jnp.bfloat16),
                 pltpu.VMEM((ROWS * PITCH, inputs), jnp.float32),
             ],
         ),
-        out_shape=[out] * (2 * slabs),
+        out_shape=[twice] * cuts + [out] * slabs,
         compiler_params=pltpu.CompilerParams(vmem_limit_bytes=48 << 20),
         cost_estimate=pl.CostEstimate(flops=flops, bytes_accessed=24 << 20, transcendentals=0),
     )(place, samples, window, table, gains)
-    return outs[:slabs], outs[slabs:]
+    return outs[:cuts], outs[cuts:][::-1]
 
 
 def pair_kernel(scale, parts, where_ref, *refs):
@@ -304,42 +308,47 @@
     table = jnp.asarray(table_rows(samples.shape[2], NCH))
     early = part == 0
 
-    def made(first, after=()):
+    def made(first, cuts, after=()):
         block, *_ = lax.optimization_barrier((samples, *after))
-        return voltage_chunk(place, block, window, table, channel_gains, first)
+        return voltage_chunk(place, block, window, table, channel_gains, first, cuts)
 
     def across(pieces, route):
-        moved = [None] * 4
-        for d in (3, 2, 1, 0):
-            moved[d] = lax.ppermute(pieces[d], "tm", route)
-        return moved
+        got = [lax.ppermute(piece, "tm", route) for piece in pieces]
+        return [piece[k] for piece in got for k in range(piece.shape[0])][::-1]
 
     def spread(pieces):
         moved = [pieces[0]]
-        for d in range(1, 4):
-            moved.append(lax.ppermute(pieces[d], "chan", [(i, i ^ d) for i in range(4)]))
+        for d in (3, 2, 1):
+            moved.insert(1, lax.ppermute(pieces[d], "chan", [(i, i ^ d) for i in range(4)]))
+        return moved
+
+    def twinned(moved):
         mine = jnp.stack(moved, 0)
         return mine, lax.ppermute(mine, "blk", [(0, 1), (1, 0)])
 
     def added(a, b):
         return (a.astype(jnp.float32) + b.astype(jnp.float32)).astype(jnp.bfloat16)
 
-    mine, far = [], []
-    ready = ()
-    for chunk in range(spectra // CHUNK):
-        other, own = made(chunk * CHUNK, ready)
-        got = across(other, [(0, 1), (1, 0)])
+    both_ways, upward = [(0, 1), (1, 0)], [(0, 1)]
+    chunks = spectra // CHUNK
+    moved, after = [], ()
+    for chunk in range(chunks):
+        other, own = made(chunk * CHUNK, 2 if chunk == 0 else 1, after)
+        got = across(other, both_ways)
         now = [jnp.where(early, own[d], got[d]) for d in range(4)]
-        other_tail, own_tail = made(spectra + chunk * CHUNK, ready + (now[3],) if chunk == 0 else ready)
-        got_tail = across(other_tail, [(0, 1)])
-        ready = (now[2], now[1])
+        if chunk == 0:
+            after = (own[0], now[3], now[2])
+        else:
+            after = (own[0], moved[0][2])
+        other_tail, own_tail = made(spectra + chunk * CHUNK, 2 if chunk == chunks - 1 else 1, after)
+        got_tail = across(other_tail, upward)
+        moved.append(spread(now))
+        after = (own_tail[0], now[1], moved[0][3])
         later = [
             jnp.where(early, added(got[d], own_tail[d]), added(own[d], got_tail[d])) for d in range(4)
         ]
-        for pieces in (now, later):
-            a, b = spread(pieces)
-            mine.append(a)
-            far.append(b)
+        moved.append(spread(later))
+    mine, far = zip(*[twinned(pieces) for pieces in moved])
     source = (block_pairs // 2) ^ chan
     elsewhere = (block_pairs % 2) ^ half
     where = jnp.stack([source, elsewhere], 2).reshape(-1).astype(jnp.int32)

time: 337 us -> 406 us (1.20)
  waiting for transfers between devices: 117 us -> 227 us
  starting transfers between devices: 91 us -> 50.6 us
    ppermute x20 -> x10, waiting for transfers between devices: 97.1 us -> 154 us  [the longest x6 150 us: across(): got = [lax.ppermute(piece, 'tm', route) for piece in pieces]]
    ppermute x12, waiting for transfers between devices: 19.6 us -> 73.7 us  [spread(): lax.ppermute(pieces[d], 'chan', [(i, i ^ d) for i in range(4)])]
    ppermute x20 -> x10, starting transfers between devices: 79.1 us -> 37.5 us  [the longest x4 30.9 us: twinned(): return (mine, lax.ppermute(mine, 'blk', [(0, 1), (1, 0)]))]
    select_n x6 -> x1, other arithmetic: 5.1 us -> 0.68 us  [quick_shards(): jnp.where(early, added(got[d], own_tail[d]), added(own[d], got_tail[d]))]
  transfers between devices with their start and end apart: 32 -> 22, of which waited for: 17 -> 11; matrix products, arithmetic and copies ran while one was open for 5% -> 3% of each run, Pallas kernels for 20% -> 11%
where the time goes in v3:
time: 406 us; the launch traced here: 404 us
  waiting for transfers between devices  227 us (56%)
  Pallas kernels  111 us (27%)
  starting transfers between devices  50.6 us (12%)
  other arithmetic  11.3 us (3%)
    ppermute x6, waiting for transfers between devices, across(): got = [lax.ppermute(piece, 'tm', route) for piece in pieces]  150 us
    pallas_call x4, Pallas kernels, voltage_chunk(): pl.pallas_call(functools.partial(voltage_kernel, first, cuts), grid_spec=...  89.3 us
    ppermute x12, waiting for transfers between devices, spread(): lax.ppermute(pieces[d], 'chan', [(i, i ^ d) for i in range(4)])  73.7 us
    ppermute x4, starting transfers between devices, twinned(): return (mine, lax.ppermute(mine, 'blk', [(0, 1), (1, 0)]))  30.9 us
    pallas_call x1, Pallas kernels, pair_products(): pl.pallas_call(functools.partial(pair_kernel, scale, parts), grid_spec=pl...  22.1 us
    ppermute x12, starting transfers between devices, spread(): lax.ppermute(pieces[d], 'chan', [(i, i ^ d) for i in range(4)])  13.2 us
    another operation x6, other arithmetic, twinned(): mine = jnp.stack(moved, 0)  9.26 us
  transfers between devices with their start and end apart: 22, of which 11 were waited for; matrix products, arithmetic and copies ran while one was open for 3% of the time, Pallas kernels for 11%

profile of v3, /device:TPU:19, one launch (start us, length us, event | category | flops | bytes accessed | tf_op | source)
XLA Modules:
  0.0 404.3 jit_solution(5602425694068210481)
XLA Ops:
  0.0 0.1 pad_add_fusion.1.place_ref
  0.1 1.2 copy-done.3
  1.3 19.9 %shard_map.55 = (bf16[2,128,16,128]{3,2,1,0:T(8,128)(2,1)}, bf16[2,128,16,128]{3,2,1,0:T(8,128)(2,1)S(1)}, bf16[128,16,128]{2,1,0:T(8,128)(2,1)S(1)}, bf16[128,1...) custom-call(s32[2]{0:T(128)S(1)} %pad_add_fusion.1.place_ref, ...), custom_call_target="tpu_custom_call" | custom-call | flops 8589934592 | bytes 25165824 | tf_op jit(solution)/shard_map/pallas_call | solution.py:218
  21.2 1.0 copy-done.1
  22.2 0.3 collective-permute-start.2
  22.5 24.1 %collective-permute-done.2 = bf16[2,128,16,128]{3,2,1,0:T(8,128)(2,1)} collective-permute-done((bf16[2,128,16,128]{3,2,1,0:T(8,128)(2,1)}, bf16[2,128,16,128]{3,2,1,0:T(8,128)(2,1)}, u32[]{:S(2)}, u32[]{:S(2)}) %collective-permute-start.2) | collective-permute-done | bytes 1048608 | tf_op jit(solution)/shard_map/ppermute | solution.py:316
  46.6 1.3 broadcast_select_fusion.4
  47.9 25.0 %shard_map.56 = (bf16[4,128,16,128]{3,2,1,0:T(8,128)(2,1)}, bf16[128,16,128]{2,1,0:T(8,128)(2,1)S(1)}, bf16[128,16,128]{2,1,0:T(8,128)(2,1)S(1)}, bf16[128,16,12...) custom-call(s32[2]{0:T(128)S(1)} %pad_add_fusion.1.place_ref, bf16[16,128,2048]{2,1,0:T(8,128)(2,1)} %x_ref.3, ...), custom_call_target="tpu_custom_call" | custom-call | flops 8589934592 | bytes 25165824 | tf_op jit(solution)/shard_map/pallas_call | solution.py:218
  72.9 1.3 collective-permute-start.5
  74.2 2.3 collective-permute-start
  76.4 0.2 collective-permute-start.4
  76.6 3.2 collective-permute-start.3
  79.8 63.2 %collective-permute-done = bf16[2,128,16,128]{3,2,1,0:T(8,128)(2,1)S(1)} collective-permute-done((bf16[2,128,16,128]{3,2,1,0:T(8,128)(2,1)S(1)}, bf16[2,128,16,128]{3,2,1,0:T(8,128)(2,1)S(1)}, u32[]{:S(2)}, u32[]{:S(2)}) %collective-permute-start) | collective-permute-done | bytes 1048608 | tf_op jit(solution)/shard_map/ppermute | solution.py:316
  143.0 0.0 collective-permute-done.5
  143.0 2.4 fusion.9
  145.4 0.0 collective-permute-done.4
  145.4 0.0 copy-start.5
  145.4 25.6 %shard_map.57 = (bf16[4,128,16,128]{3,2,1,0:T(8,128)(2,1)}, bf16[128,16,128]{2,1,0:T(8,128)(2,1)S(1)}, bf16[128,16,128]{2,1,0:T(8,128)(2,1)S(1)}, bf16[128,16,12...) custom-call(s32[2]{0:T(128)S(1)} %pad_add_fusion.1.place_ref, bf16[16,128,2048]{2,1,0:T(8,128)(2,1)} %x_ref.3, ...), custom_call_target="tpu_custom_call" | custom-call | flops 8589934592 | bytes 25165824 | tf_op jit(solution)/shard_map/pallas_call | solution.py:218
  171.0 0.0 collective-permute-start.9
  171.0 0.0 collective-permute-done.3
  171.0 18.8 %shard_map.58 = (bf16[2,128,16,128]{3,2,1,0:T(8,128)(2,1)S(1)}, bf16[2,128,16,128]{3,2,1,0:T(8,128)(2,1)S(1)}, bf16[128,16,128]{2,1,0:T(8,128)(2,1)S(1)}, bf16[1...) custom-call(s32[2]{0:T(128)S(1)} %pad_add_fusion.1.place_ref, ...), custom_call_target="tpu_custom_call" | custom-call | flops 8589934592 | bytes 25165824 | tf_op jit(solution)/shard_map/pallas_call | solution.py:218
  189.8 1.3 collective-permute-start.13
  191.1 1.5 collective-permute-start.15
  192.6 1.4 collective-permute-start.1
  194.0 0.2 collective-permute-start.6
  194.2 44.2 %collective-permute-done.13 = bf16[2,128,16,128]{3,2,1,0:T(8,128)(2,1)S(1)} collective-permute-done((bf16[2,128,16,128]{3,2,1,0:T(8,128)(2,1)S(1)}, bf16[2,128,16,128]{3,2,1,0:T(8,128)(2,1)S(1)}, u32[]{:S(2)}, u32[]{:S(2)}) %collective-permute-start.13) | collective-permute-done | bytes 1048608 | tf_op jit(solution)/shard_map/ppermute | solution.py:316
  238.3 0.2 collective-permute-start.8
  238.5 0.0 collective-permute-done.9
  238.5 3.2 collective-permute-start.7
  241.8 0.7 fusion.14
  242.4 18.4 %collective-permute-done.15 = bf16[2,128,16,128]{3,2,1,0:T(8,128)(2,1)S(1)} collective-permute-done((bf16[2,128,16,128]{3,2,1,0:T(8,128)(2,1)S(1)}, bf16[2,128,16,128]{3,2,1,0:T(8,128)(2,1)S(1)}, u32[]{:S(2)}, u32[]{:S(2)}) %collective-permute-start.15) | collective-permute-done | bytes 1048608 | tf_op jit(solution)/shard_map/ppermute | solution.py:316
  260.8 1.3 collective-permute-start.10
  262.1 0.7 fusion.16
  262.8 0.0 collective-permute-done.6
  262.8 0.1 collective-permute-start.12
  262.9 10.3 %collective-permute-done.8 = bf16[128,16,128]{2,1,0:T(8,128)(2,1)S(1)} collective-permute-done((bf16[128,16,128]{2,1,0:T(8,128)(2,1)S(1)}, bf16[128,16,128]{2,1,0:T(8,128)(2,1)S(1)}, u32[]{:S(2)}, u32[]{:S(2)}) %collective-permute-start.8) | collective-permute-done | bytes 524320 | tf_op jit(solution)/shard_map/ppermute | solution.py:322
  273.2 0.0 collective-permute-start.11
  273.2 32.3 %collective-permute-done.7 = bf16[128,16,128]{2,1,0:T(8,128)(2,1)S(1)} collective-permute-done((bf16[128,16,128]{2,1,0:T(8,128)(2,1)S(1)}, bf16[128,16,128]{2,1,0:T(8,128)(2,1)S(1)}, u32[]{:S(2)}, u32[]{:S(2)}) %collective-permute-start.7) | collective-permute-done | bytes 524320 | tf_op jit(solution)/shard_map/ppermute | solution.py:322
  305.4 2.1 collective-permute-start.14
  307.5 0.0 collective-permute-done.1
  307.6 1.0 collective-permute-start.16
  308.6 0.0 collective-permute-done.10
  308.6 0.3 collective-permute-start.17
  308.9 0.3 pad_maximum_fusion.1.refs_1_.refs_9_
  309.2 0.8 copy-done.6
  309.9 2.7 pad_maximum_fusion.refs_0_.refs_8_
  312.6 6.1 %collective-permute-done.12 = bf16[128,16,128]{2,1,0:T(8,128)(2,1)S(1)} collective-permute-done((bf16[128,16,128]{2,1,0:T(8,128)(2,1)S(1)}, bf16[128,16,128]{2,1,0:T(8,128)(2,1)S(1)}, u32[]{:S(2)}, u32[]{:S(2)}) %collective-permute-start.12) | collective-permute-done | bytes 524320 | tf_op jit(solution)/shard_map/ppermute | solution.py:322
  318.7 26.0 %collective-permute-start.18 = (bf16[4,128,16,128]{3,2,1,0:T(8,128)(2,1)}, bf16[4,128,16,128]{3,2,1,0:T(8,128)(2,1)}, u32[]{:S(2)}, u32[]{:S(2)}) collective-permute-start(bf16[4,128,16,128]{3,2,1,0:T(8,128)(2,1)} %pad_maximum_fusion.refs_0_.refs_8_), channel_id=1, source_target_pairs={{0,1},{1,0},{2,3},{3,2},{4,5},{5,4},{6,7},{7,6},{8,9},{9,8},{10,11... | collective-permute-start | bytes 6291464 | tf_op jit(solution)/shard_map/ppermute | solution.py:327
  344.7 5.7 %collective-permute-done.11 = bf16[128,16,128]{2,1,0:T(8,128)(2,1)S(1)} collective-permute-done((bf16[128,16,128]{2,1,0:T(8,128)(2,1)S(1)}, bf16[128,16,128]{2,1,0:T(8,128)(2,1)S(1)}, u32[]{:S(2)}, u32[]{:S(2)}) %collective-permute-start.11) | collective-permute-done | bytes 524320 | tf_op jit(solution)/shard_map/ppermute | solution.py:322
  350.4 2.4 collective-permute-start.19
  352.8 1.6 pad_maximum_fusion.2.refs_2_.refs_10_
  354.4 0.0 collective-permute-done.14
  354.4 0.0 collective-permute-start.20
  354.4 7.2 %collective-permute-done.16 = bf16[128,16,128]{2,1,0:T(8,128)(2,1)S(1)} collective-permute-done((bf16[128,16,128]{2,1,0:T(8,128)(2,1)S(1)}, bf16[128,16,128]{2,1,0:T(8,128)(2,1)S(1)}, u32[]{:S(2)}, u32[]{:S(2)}) %collective-permute-start.16) | collective-permute-done | bytes 524320 | tf_op jit(solution)/shard_map/ppermute | solution.py:322
  361.6 12.2 %collective-permute-done.17 = bf16[128,16,128]{2,1,0:T(8,128)(2,1)S(1)} collective-permute-done((bf16[128,16,128]{2,1,0:T(8,128)(2,1)S(1)}, bf16[128,16,128]{2,1,0:T(8,128)(2,1)S(1)}, u32[]{:S(2)}, u32[]{:S(2)}) %collective-permute-start.17) | collective-permute-done | bytes 524320 | tf_op jit(solution)/shard_map/ppermute | solution.py:322
  373.8 1.6 pad_maximum_fusion.3.refs_3_.refs_11_
  375.4 2.5 collective-permute-start.21
  377.9 0.1 copy.6
  378.0 0.1 reshape.19.where_ref
  378.1 0.0 collective-permute-done.18.refs_4_.refs_12_
  378.1 0.0 collective-permute-done.19.refs_5_.refs_13_
  378.1 0.0 collective-permute-done.20.refs_6_.refs_14_
  378.1 3.9 collective-permute-done.21.refs_7_.refs_15_
  382.0 22.1 %shard_map.59 = f32[2,128,2,128,128]{4,3,2,1,0:T(8,128)} custom-call(s32[8]{0:T(128)S(1)} %reshape.19.where_ref, bf16[4,128,16,128]{3,2,1,0:T(8,128)(2,1)} %pad_maximum_fusion.refs_0_.refs_8_, bf16[4,128,16,128]{3,2,1,0:T(8,128)(2,1)S(1)} %pad_maximum_fusion.1.refs_1_.refs_9_, bf16[4,128,16,128]{3,2,1,0:T(8,128)(2,1)} %pad_maximum_fusion.2.refs_2_.refs_10_, ...), custom_call_target="tpu_custom_call" | custom-call | flops 4294967296 | bytes 52428800 | tf_op jit(solution)/shard_map/pallas_call | solution.py:289
  (14 shorter events, 0.0 us)
Async XLA Ops:
  0.1 1.2 copy-start.3
  21.2 1.0 copy-start.1
  22.2 25.7 %copy-start = (f32[2,1024,128]{2,1,0:T(8,128)S(1)}, f32[2,1024,128]{2,1,0:T(8,128)}, u32[]{:S(2)}) copy-start(f32[2,1024,128]{2,1,0:T(8,128)} %gain_ref.7) | copy-start | bytes 3145732
  22.2 24.3 %collective-permute-start.2 = (bf16[2,128,16,128]{3,2,1,0:T(8,128)(2,1)}, bf16[2,128,16,128]{3,2,1,0:T(8,128)(2,1)}, u32[]{:S(2)}, u32[]{:S(2)}) collective-permute-start(bf16[2,128,16,128]{3,2,1,0:T(8,128)(2,1)} %get-tuple-element.34), channel_id=1, source_target_pairs={{0,2},{2,0},{1,3},{3,1},{4,6},{6,4},{5,7},{7,5},{8,10},{10,8},{9,1... | collective-permute-start | bytes 3145736 | tf_op jit(solution)/shard_map/ppermute | solution.py:316
  22.5 25.4 %copy-start.4 = (f32[16,8,2048]{2,1,0:T(8,128)S(1)}, f32[16,8,2048]{2,1,0:T(8,128)}, u32[]{:S(2)}) copy-start(f32[16,8,2048]{2,1,0:T(8,128)} %constant.42.clone.w_ref) | copy-start | bytes 3145732
  47.9 26.3 %copy-start.2 = (bf16[2,128,16,128]{3,2,1,0:T(8,128)(2,1)S(1)}, bf16[2,128,16,128]{3,2,1,0:T(8,128)(2,1)}, u32[]{:S(2)}) copy-start(bf16[2,128,16,128]{3,2,1,0:T(8,128)(2,1)} %copy-done.1) | copy-start | bytes 3145732
  72.9 70.1 %collective-permute-start.5 = (bf16[4,128,16,128]{3,2,1,0:T(8,128)(2,1)}, bf16[4,128,16,128]{3,2,1,0:T(8,128)(2,1)S(1)}, u32[]{:S(2)}, u32[]{:S(2)}) collective-permute-start(bf16[4,128,16,128]{3,2,1,0:T(8,128)(2,1)} %get-tuple-element.38), channel_id=1, source_target_pairs={{0,2},{1,3},{4,6},{5,7},{8,10},{9,11},{12,14},{13,15},{16,18},{17,... | collective-permute-start | bytes 6291464 | tf_op jit(solution)/shard_map/ppermute | solution.py:316
  74.2 68.8 %collective-permute-start = (bf16[2,128,16,128]{3,2,1,0:T(8,128)(2,1)S(1)}, bf16[2,128,16,128]{3,2,1,0:T(8,128)(2,1)S(1)}, u32[]{:S(2)}, u32[]{:S(2)}) collective-permute-start(bf16[2,128,16,128]{3,2,1,0:T(8,128)(2,1)S(1)} %copy-done.2), channel_id=1, source_target_pairs={{0,2},{2,0},{1,3},{3,1},{4,6},{6,4},{5,7},{7,5},{8,10},{10,8},{9,1... | collective-permute-start | bytes 3145736 | tf_op jit(solution)/shard_map/ppermute | solution.py:316
  76.4 69.0 %collective-permute-start.4 = (bf16[128,16,128]{2,1,0:T(8,128)(2,1)S(1)}, bf16[128,16,128]{2,1,0:T(8,128)(2,1)S(1)}, u32[]{:S(2)}, u32[]{:S(2)}) collective-permute-start(bf16[128,16,128]{2,1,0:T(8,128)(2,1)S(1)} %get-tuple-element.72), channel_id=1, source_target_pairs={{0,12},{4,8},{8,4},{12,0},{1,13},{5,9},{9,5},{13,1},{2,14},{6,10},... | collective-permute-start | bytes 1572872 | tf_op jit(solution)/shard_map/ppermute | solution.py:322
  76.6 94.4 %collective-permute-start.3 = (bf16[128,16,128]{2,1,0:T(8,128)(2,1)S(1)}, bf16[128,16,128]{2,1,0:T(8,128)(2,1)}, u32[]{:S(2)}, u32[]{:S(2)}) collective-permute-start(bf16[128,16,128]{2,1,0:T(8,128)(2,1)S(1)} %get-tuple-element.71), channel_id=1, source_target_pairs={{0,8},{4,12},{8,0},{12,4},{1,9},{5,13},{9,1},{13,5},{2,10},{6,14},... | collective-permute-start | bytes 1572872 | tf_op jit(solution)/shard_map/ppermute | solution.py:322
  145.4 25.6 %copy-start.5 = (bf16[128,16,128]{2,1,0:T(8,128)(2,1)}, bf16[128,16,128]{2,1,0:T(8,128)(2,1)S(1)}, u32[]{:S(2)}) copy-start(bf16[128,16,128]{2,1,0:T(8,128)(2,1)S(1)} %collective-permute-done.4) | copy-start | bytes 1572868
  171.0 67.5 %collective-permute-start.9 = (bf16[4,128,16,128]{3,2,1,0:T(8,128)(2,1)}, bf16[4,128,16,128]{3,2,1,0:T(8,128)(2,1)S(1)}, u32[]{:S(2)}, u32[]{:S(2)}) collective-permute-start(bf16[4,128,16,128]{3,2,1,0:T(8,128)(2,1)} %get-tuple-element.44), channel_id=1, source_target_pairs={{0,2},{2,0},{1,3},{3,1},{4,6},{6,4},{5,7},{7,5},{8,10},{10,8},{9,1... | collective-permute-start | bytes 6291464 | tf_op jit(solution)/shard_map/ppermute | solution.py:316
  189.8 48.5 %collective-permute-start.13 = (bf16[2,128,16,128]{3,2,1,0:T(8,128)(2,1)S(1)}, bf16[2,128,16,128]{3,2,1,0:T(8,128)(2,1)S(1)}, u32[]{:S(2)}, u32[]{:S(2)}) collective-permute-start(bf16[2,128,16,128]{3,2,1,0:T(8,128)(2,1)S(1)} %get-tuple-element.50), channel_id=1, source_target_pairs={{0,2},{1,3},{4,6},{5,7},{8,10},{9,11},{12,14},{13,15},{16,18},{17,... | collective-permute-start | bytes 3145736 | tf_op jit(solution)/shard_map/ppermute | solution.py:316
  191.1 69.7 %collective-permute-start.15 = (bf16[2,128,16,128]{3,2,1,0:T(8,128)(2,1)S(1)}, bf16[2,128,16,128]{3,2,1,0:T(8,128)(2,1)S(1)}, u32[]{:S(2)}, u32[]{:S(2)}) collective-permute-start(bf16[2,128,16,128]{3,2,1,0:T(8,128)(2,1)S(1)} %get-tuple-element.53), channel_id=1, source_target_pairs={{0,2},{1,3},{4,6},{5,7},{8,10},{9,11},{12,14},{13,15},{16,18},{17,... | collective-permute-start | bytes 3145736 | tf_op jit(solution)/shard_map/ppermute | solution.py:316
  192.6 114.9 %collective-permute-start.1 = (bf16[128,16,128]{2,1,0:T(8,128)(2,1)S(1)}, bf16[128,16,128]{2,1,0:T(8,128)(2,1)S(1)}, u32[]{:S(2)}, u32[]{:S(2)}) collective-permute-start(bf16[128,16,128]{2,1,0:T(8,128)(2,1)S(1)} %get-tuple-element.69), channel_id=1, source_target_pairs={{0,4},{4,0},{8,12},{12,8},{1,5},{5,1},{9,13},{13,9},{2,6},{6,2},{1... | collective-permute-start | bytes 1572872 | tf_op jit(solution)/shard_map/ppermute | solution.py:322
  194.0 68.8 %collective-permute-start.6 = (bf16[128,16,128]{2,1,0:T(8,128)(2,1)S(1)}, bf16[128,16,128]{2,1,0:T(8,128)(2,1)S(1)}, u32[]{:S(2)}, u32[]{:S(2)}) collective-permute-start(bf16[128,16,128]{2,1,0:T(8,128)(2,1)S(1)} %get-tuple-element.60), channel_id=1, source_target_pairs={{0,4},{4,0},{8,12},{12,8},{1,5},{5,1},{9,13},{13,9},{2,6},{6,2},{1... | collective-permute-start | bytes 1572872 | tf_op jit(solution)/shard_map/ppermute | solution.py:322
  238.3 34.8 %collective-permute-start.8 = (bf16[128,16,128]{2,1,0:T(8,128)(2,1)S(1)}, bf16[128,16,128]{2,1,0:T(8,128)(2,1)S(1)}, u32[]{:S(2)}, u32[]{:S(2)}) collective-permute-start(bf16[128,16,128]{2,1,0:T(8,128)(2,1)S(1)} %get-tuple-element.67), channel_id=1, source_target_pairs={{0,12},{4,8},{8,4},{12,0},{1,13},{5,9},{9,5},{13,1},{2,14},{6,10},... | collective-permute-start | bytes 1572872 | tf_op jit(solution)/shard_map/ppermute | solution.py:322
  238.5 66.9 %collective-permute-start.7 = (bf16[128,16,128]{2,1,0:T(8,128)(2,1)S(1)}, bf16[128,16,128]{2,1,0:T(8,128)(2,1)S(1)}, u32[]{:S(2)}, u32[]{:S(2)}) collective-permute-start(bf16[128,16,128]{2,1,0:T(8,128)(2,1)S(1)} %get-tuple-element.68), channel_id=1, source_target_pairs={{0,8},{4,12},{8,0},{12,4},{1,9},{5,13},{9,1},{13,5},{2,10},{6,14},... | collective-permute-start | bytes 1572872 | tf_op jit(solution)/shard_map/ppermute | solution.py:322
  260.8 47.7 %collective-permute-start.10 = (bf16[128,16,128]{2,1,0:T(8,128)(2,1)S(1)}, bf16[128,16,128]{2,1,0:T(8,128)(2,1)S(1)}, u32[]{:S(2)}, u32[]{:S(2)}) collective-permute-start(bf16[128,16,128]{2,1,0:T(8,128)(2,1)S(1)} %get-tuple-element.64), channel_id=1, source_target_pairs={{0,4},{4,0},{8,12},{12,8},{1,5},{5,1},{9,13},{13,9},{2,6},{6,2},{1... | collective-permute-start | bytes 1572872 | tf_op jit(solution)/shard_map/ppermute | solution.py:322
  262.8 55.9 %collective-permute-start.12 = (bf16[128,16,128]{2,1,0:T(8,128)(2,1)S(1)}, bf16[128,16,128]{2,1,0:T(8,128)(2,1)S(1)}, u32[]{:S(2)}, u32[]{:S(2)}) collective-permute-start(bf16[128,16,128]{2,1,0:T(8,128)(2,1)S(1)} %get-tuple-element.63), channel_id=1, source_target_pairs={{0,12},{4,8},{8,4},{12,0},{1,13},{5,9},{9,5},{13,1},{2,14},{6,10},... | collective-permute-start | bytes 1572872 | tf_op jit(solution)/shard_map/ppermute | solution.py:322
  273.2 77.2 %collective-permute-start.11 = (bf16[128,16,128]{2,1,0:T(8,128)(2,1)S(1)}, bf16[128,16,128]{2,1,0:T(8,128)(2,1)S(1)}, u32[]{:S(2)}, u32[]{:S(2)}) collective-permute-start(bf16[128,16,128]{2,1,0:T(8,128)(2,1)S(1)} %get-tuple-element.66), channel_id=1, source_target_pairs={{0,8},{4,12},{8,0},{12,4},{1,9},{5,13},{9,1},{13,5},{2,10},{6,14},... | collective-permute-start | bytes 1572872 | tf_op jit(solution)/shard_map/ppermute | solution.py:322
  305.4 49.0 %collective-permute-start.14 = (bf16[128,16,128]{2,1,0:T(8,128)(2,1)S(1)}, bf16[128,16,128]{2,1,0:T(8,128)(2,1)S(1)}, u32[]{:S(2)}, u32[]{:S(2)}) collective-permute-start(bf16[128,16,128]{2,1,0:T(8,128)(2,1)S(1)} %get-tuple-element.56), channel_id=1, source_target_pairs={{0,4},{4,0},{8,12},{12,8},{1,5},{5,1},{9,13},{13,9},{2,6},{6,2},{1... | collective-permute-start | bytes 1572872 | tf_op jit(solution)/shard_map/ppermute | solution.py:322
  307.6 54.1 %collective-permute-start.16 = (bf16[128,16,128]{2,1,0:T(8,128)(2,1)S(1)}, bf16[128,16,128]{2,1,0:T(8,128)(2,1)S(1)}, u32[]{:S(2)}, u32[]{:S(2)}) collective-permute-start(bf16[128,16,128]{2,1,0:T(8,128)(2,1)S(1)} %get-tuple-element.57), channel_id=1, source_target_pairs={{0,8},{4,12},{8,0},{12,4},{1,9},{5,13},{9,1},{13,5},{2,10},{6,14},... | collective-permute-start | bytes 1572872 | tf_op jit(solution)/shard_map/ppermute | solution.py:322
  308.6 65.2 %collective-permute-start.17 = (bf16[128,16,128]{2,1,0:T(8,128)(2,1)S(1)}, bf16[128,16,128]{2,1,0:T(8,128)(2,1)S(1)}, u32[]{:S(2)}, u32[]{:S(2)}) collective-permute-start(bf16[128,16,128]{2,1,0:T(8,128)(2,1)S(1)} %get-tuple-element.58), channel_id=1, source_target_pairs={{0,12},{4,8},{8,4},{12,0},{1,13},{5,9},{9,5},{13,1},{2,14},{6,10},... | collective-permute-start | bytes 1572872 | tf_op jit(solution)/shard_map/ppermute | solution.py:322
  308.9 1.0 copy-start.6
  318.7 59.4 %collective-permute-start.18 = (bf16[4,128,16,128]{3,2,1,0:T(8,128)(2,1)}, bf16[4,128,16,128]{3,2,1,0:T(8,128)(2,1)}, u32[]{:S(2)}, u32[]{:S(2)}) collective-permute-start(bf16[4,128,16,128]{3,2,1,0:T(8,128)(2,1)} %pad_maximum_fusion.refs_0_.refs_8_), channel_id=1, source_target_pairs={{0,1},{1,0},{2,3},{3,2},{4,5},{5,4},{6,7},{7,6},{8,9},{9,8},{10,11... | collective-permute-start | bytes 6291464 | tf_op jit(solution)/shard_map/ppermute | solution.py:327
  350.4 27.7 %collective-permute-start.19 = (bf16[4,128,16,128]{3,2,1,0:T(8,128)(2,1)S(1)}, bf16[4,128,16,128]{3,2,1,0:T(8,128)(2,1)}, u32[]{:S(2)}, u32[]{:S(2)}) collective-permute-start(bf16[4,128,16,128]{3,2,1,0:T(8,128)(2,1)S(1)} %pad_maximum_fusion.1.refs_1_.refs_9_), channel_id=1, source_target_pairs={{0,1},{1,0},{2,3},{3,2},{4,5},{5,4},{6,7},{7,6},{8,9},{9,8},{10,11... | collective-permute-start | bytes 6291464 | tf_op jit(solution)/shard_map/ppermute | solution.py:327
  354.4 23.7 %collective-permute-start.20 = (bf16[4,128,16,128]{3,2,1,0:T(8,128)(2,1)}, bf16[4,128,16,128]{3,2,1,0:T(8,128)(2,1)}, u32[]{:S(2)}, u32[]{:S(2)}) collective-permute-start(bf16[4,128,16,128]{3,2,1,0:T(8,128)(2,1)} %pad_maximum_fusion.2.refs_2_.refs_10_), channel_id=1, source_target_pairs={{0,1},{1,0},{2,3},{3,2},{4,5},{5,4},{6,7},{7,6},{8,9},{9,8},{10,11... | collective-permute-start | bytes 6291464 | tf_op jit(solution)/shard_map/ppermute | solution.py:327
  373.8 4.1 %copy-start.7 = (s32[2,2]{1,0:T(2,128)S(1)}, s32[2,2]{1,0:T(2,128)}, u32[]{:S(2)}) copy-start(s32[2,2]{1,0:T(2,128)} %param.7) | copy-start | bytes 52
  375.4 6.6 %collective-permute-start.21 = (bf16[4,128,16,128]{3,2,1,0:T(8,128)(2,1)}, bf16[4,128,16,128]{3,2,1,0:T(8,128)(2,1)}, u32[]{:S(2)}, u32[]{:S(2)}) collective-permute-start(bf16[4,128,16,128]{3,2,1,0:T(8,128)(2,1)} %pad_maximum_fusion.3.refs_3_.refs_11_), channel_id=1, source_target_pairs={{0,1},{1,0},{2,3},{3,2},{4,5},{5,4},{6,7},{7,6},{8,9},{9,8},{10,11... | collective-permute-start | bytes 6291464 | tf_op jit(solution)/shard_map/ppermute | solution.py:327
